TPU v7x, 32 devices: a whole 2x2x4 slice. The times are simulated.
32 devices in a mesh: dp: 4 (over z), context: 2 (over y), tensor: 4 (over x, core).
Axes of the slice: x: 2, y: 2, z: 4, core: 2. Of those that a mesh axis runs over, the one named last changes fastest.
Arguments:
- tokens: bfloat16 [4, 1024, 1024], P('dp', 'context'), may hold values from -6 to 6
- key_valid: int32 [4, 1024], P('dp', 'context'), may hold values from 0 to 1, as said below
- norm1_gain: bfloat16 [1024], P(('dp', 'context')), may hold values from 0.25 to 1.75
- norm1_shift: bfloat16 [1024], P(('dp', 'context')), may hold values from -4 to 4
- w_qkv: bfloat16 [1024, 3, 1024], P(('dp', 'context'), None, 'tensor'), may hold values from -0.25 to 0.25
- qv_bias: bfloat16 [2, 1024], P(None, ('tensor', 'dp', 'context')), may hold values from -4 to 4
- w_out: bfloat16 [1024, 1024], P('tensor', ('dp', 'context')), may hold values from -0.75 to 0.75
- out_bias: bfloat16 [1024], P(('dp', 'context')), may hold values from -4 to 4
- scale1: bfloat16 [1024], P(('dp', 'context')), may hold values from 0.5 to 1.5
- norm2_gain: bfloat16 [1024], P(('dp', 'context')), may hold values from 0.25 to 1.75
- norm2_shift: bfloat16 [1024], P(('dp', 'context')), may hold values from -4 to 4
- w_fc1: bfloat16 [1024, 4096], P(('dp', 'context'), 'tensor'), may hold values from -0.1875 to 0.1875
- fc1_bias: bfloat16 [4096], P(('tensor', 'dp', 'context')), may hold values from -4 to 4
- w_fc2: bfloat16 [4096, 1024], P('tensor', ('dp', 'context')), may hold values from -0.125 to 0.125
- fc2_bias: bfloat16 [1024], P(('dp', 'context')), may hold values from -4 to 4
- scale2: bfloat16 [1024], P(('dp', 'context')), may hold values from 0.5 to 1.5
- cotangent: bfloat16 [4, 1024, 1024], P('dp', 'context'), may hold values from -6 to 6
Outputs:
- block_out: bfloat16 [4, 1024, 1024], P('dp', 'context')
- token_grad: float32 [4, 1024, 1024], P('dp', 'context')
- norm1_gain_grad: float32 [1024], P(('dp', 'context'))
- norm1_shift_grad: float32 [1024], P(('dp', 'context'))
- w_qkv_grad: float32 [1024, 3, 1024], P(('dp', 'context'), None, 'tensor')
- qv_bias_grad: float32 [2, 1024], P(None, ('tensor', 'dp', 'context'))
- w_out_grad: float32 [1024, 1024], P('tensor', ('dp', 'context'))
- out_bias_grad: float32 [1024], P(('dp', 'context'))
- scale1_grad: float32 [1024], P(('dp', 'context'))
- norm2_gain_grad: float32 [1024], P(('dp', 'context'))
- norm2_shift_grad: float32 [1024], P(('dp', 'context'))
- w_fc1_grad: float32 [1024, 4096], P(('dp', 'context'), 'tensor')
- fc1_bias_grad: float32 [4096], P(('tensor', 'dp', 'context'))
- w_fc2_grad: float32 [4096, 1024], P('tensor', ('dp', 'context'))
- fc2_bias_grad: float32 [1024], P(('dp', 'context'))
- scale2_grad: float32 [1024], P(('dp', 'context'))
Inputs may be any that keep to these rules, and one draw needn't show every extreme that they name: In each image the tokens with key_valid 1 come first; one or more padded tokens with key_valid 0 follow them.
All inputs are finite; a program needn't handle non-finite values.
Results may differ from a plain program's by a relative error of at most 0.02.
Values may be sent and summed in bfloat16 or wider, within the bound.
A program may use at most 128 MiB of HBM per device.

v0:
```python
import jax
import jax.numpy as jnp
from jax import lax
from jax.sharding import PartitionSpec as P

HEAD_DIM = 64


EPSILON = 1e-06
NEGATIVE = -1e30


def normalize(value):
    average = jnp.mean(value, axis=-1, keepdims=True)
    centred = value - average
    inv_std = lax.rsqrt(jnp.mean(centred * centred, axis=-1, keepdims=True) + EPSILON)
    return (centred * inv_std, inv_std)


def norm_backward(grad_norm, normed, inv_std, gain):
    scaled = grad_norm * gain
    return (
        scaled
        - jnp.mean(scaled, axis=-1, keepdims=True)
        - normed * jnp.mean(scaled * normed, axis=-1, keepdims=True)
    ) * inv_std


def contract_rows(first_matrix, second_matrix):
    return lax.dot_general(
        first_matrix, second_matrix, (((0,), (0,)), ((), ())), preferred_element_type=jnp.float32
    )


def contract_cols(first_matrix, second_matrix):
    return lax.dot_general(
        first_matrix, second_matrix, (((1,), (1,)), ((), ())), preferred_element_type=jnp.float32
    )


def attend(carry, query_heads, key_rows, value_rows, key_mask):
    running_max, running_total, running_sum = carry
    key_count = key_rows.shape[0]
    head_count = query_heads.shape[1]
    for offset in range(0, key_count, 512):
        finish = min(key_count, offset + 512)
        key_block = key_rows[offset:finish].reshape(finish - offset, head_count, HEAD_DIM)
        value_block = value_rows[offset:finish].reshape(finish - offset, head_count, HEAD_DIM)
        mask_block = key_mask[offset:finish][None, None, :] > 0
        scores = jnp.einsum(
            "rhe,nhe->rhn", query_heads, key_block, preferred_element_type=jnp.float32
        ) * HEAD_DIM ** (-0.5)
        scores = jnp.where(mask_block, scores, NEGATIVE)
        new_max = jnp.maximum(running_max, jnp.max(scores, axis=-1, keepdims=True))
        weights = jnp.where(mask_block, jnp.exp(scores - new_max), 0.0)
        factor = jnp.exp(running_max - new_max)
        running_total = running_total * factor + jnp.sum(weights, axis=-1, keepdims=True)
        running_sum = running_sum * factor + jnp.einsum(
            "rhn,nhe->rhe",
            weights.astype(jnp.bfloat16),
            value_block,
            preferred_element_type=jnp.float32,
        )
        running_max = new_max
    return (running_max, running_total, running_sum)


def on_device(
    tokens,
    key_valid,
    norm1_gain,
    norm1_shift,
    w_qkv,
    qv_bias,
    w_out,
    out_bias,
    scale1,
    norm2_gain,
    norm2_shift,
    w_fc1,
    fc1_bias,
    w_fc2,
    fc2_bias,
    scale2,
    cotangent,
):
    gathered = (
        lax.all_gather(norm1_gain, ("dp", "context"), axis=0, tiled=True),
        lax.all_gather(norm1_shift, ("dp", "context"), axis=0, tiled=True),
        lax.all_gather(w_qkv, ("dp", "context"), axis=0, tiled=True),
        lax.all_gather(qv_bias, ("dp", "context"), axis=1, tiled=True),
        lax.all_gather(w_out, ("dp", "context"), axis=1, tiled=True),
        lax.all_gather(out_bias, ("dp", "context"), axis=0, tiled=True),
        lax.all_gather(scale1, ("dp", "context"), axis=0, tiled=True),
        lax.all_gather(norm2_gain, ("dp", "context"), axis=0, tiled=True),
        lax.all_gather(norm2_shift, ("dp", "context"), axis=0, tiled=True),
        lax.all_gather(w_fc1, ("dp", "context"), axis=0, tiled=True),
        lax.all_gather(fc1_bias, ("dp", "context"), axis=0, tiled=True),
        lax.all_gather(w_fc2, ("dp", "context"), axis=1, tiled=True),
        lax.all_gather(fc2_bias, ("dp", "context"), axis=0, tiled=True),
        lax.all_gather(scale2, ("dp", "context"), axis=0, tiled=True),
    )
    (
        gain_one,
        shift_one,
        qkv_full,
        qv_full,
        out_full,
        bias_out,
        scale_one,
        gain_two,
        shift_two,
        fc1_full,
        bias_fc1,
        fc2_full,
        bias_fc2,
        scale_two,
    ) = gathered
    gain_one = gain_one.astype(jnp.float32)
    shift_one = shift_one.astype(jnp.float32)
    bias_out = bias_out.astype(jnp.float32)
    scale_one = scale_one.astype(jnp.float32)
    gain_two = gain_two.astype(jnp.float32)
    shift_two = shift_two.astype(jnp.float32)
    bias_fc1 = bias_fc1.astype(jnp.float32)
    bias_fc2 = bias_fc2.astype(jnp.float32)
    scale_two = scale_two.astype(jnp.float32)
    qv_float = qv_full.astype(jnp.float32)
    residual = tokens[0].astype(jnp.float32)
    row_count = residual.shape[0]
    model_width = residual.shape[1]
    local_width = qkv_full.shape[2]
    head_count = local_width // HEAD_DIM
    normed_one, inv_one = normalize(residual)
    hidden_one = (normed_one * gain_one + shift_one).astype(jnp.bfloat16)
    projected = jnp.dot(
        hidden_one,
        qkv_full.reshape(model_width, 3 * local_width),
        preferred_element_type=jnp.float32,
    ).reshape(row_count, 3, local_width)
    queries = (projected[:, 0] + qv_float[0]).astype(jnp.bfloat16)
    key_rows = projected[:, 1].astype(jnp.bfloat16)
    values = (projected[:, 2] + qv_float[1]).astype(jnp.bfloat16)
    query_heads = queries.reshape(row_count, head_count, HEAD_DIM)
    key_mask = key_valid[0].astype(jnp.bfloat16)
    start_carry = (
        jnp.full((row_count, head_count, 1), NEGATIVE, jnp.float32),
        jnp.zeros((row_count, head_count, 1), jnp.float32),
        jnp.zeros((row_count, head_count, HEAD_DIM), jnp.float32),
    )
    running_max, running_total, running_sum = attend(
        start_carry,
        query_heads,
        lax.all_gather(key_rows, "context", axis=0, tiled=True),
        lax.all_gather(values, "context", axis=0, tiled=True),
        lax.all_gather(key_mask, "context", axis=0, tiled=True),
    )
    attn_heads = running_sum / running_total
    log_total = running_max + jnp.log(running_total)
    attended = attn_heads.reshape(row_count, local_width).astype(jnp.bfloat16)
    branch = (
        lax.psum(
            jnp.dot(attended, out_full, preferred_element_type=jnp.float32).astype(jnp.bfloat16),
            "tensor",
        ).astype(jnp.float32)
        + bias_out
    )
    residual_one = residual + scale_one * branch
    normed_two, inv_two = normalize(residual_one)
    hidden_two = (normed_two * gain_two + shift_two).astype(jnp.bfloat16)
    pre_act = jnp.dot(hidden_two, fc1_full, preferred_element_type=jnp.float32) + bias_fc1
    activated, gelu_pull = jax.vjp(lambda value: jax.nn.gelu(value, approximate=False), pre_act)
    hidden = activated.astype(jnp.bfloat16)
    mlp_out = (
        lax.psum(
            jnp.dot(hidden, fc2_full, preferred_element_type=jnp.float32).astype(jnp.bfloat16),
            "tensor",
        ).astype(jnp.float32)
        + bias_fc2
    )
    block_out = (residual_one + scale_two * mlp_out).astype(jnp.bfloat16)
    back_weights = (
        lax.all_gather(w_qkv, ("dp", "context"), axis=0, tiled=True),
        lax.all_gather(w_out, ("dp", "context"), axis=1, tiled=True),
        lax.all_gather(w_fc1, ("dp", "context"), axis=0, tiled=True),
        lax.all_gather(w_fc2, ("dp", "context"), axis=1, tiled=True),
    )
    qkv_back, out_back, fc1_back, fc2_back = back_weights
    grad_out = cotangent[0].astype(jnp.float32)
    grad_scale_two = jnp.sum(grad_out * mlp_out, axis=0)
    grad_mlp = (grad_out * scale_two).astype(jnp.bfloat16)
    grad_bias_fc2 = jnp.sum(grad_mlp.astype(jnp.float32), axis=0)
    grad_fc2 = contract_rows(hidden, grad_mlp)
    grad_act = contract_cols(grad_mlp, fc2_back)
    grad_pre = gelu_pull(grad_act)[0].astype(jnp.bfloat16)
    grad_bias_fc1 = jnp.sum(grad_pre.astype(jnp.float32), axis=0)
    grad_fc1 = contract_rows(hidden_two, grad_pre)
    grad_hidden_two = lax.psum(
        contract_cols(grad_pre, fc1_back).astype(jnp.bfloat16), "tensor"
    ).astype(jnp.float32)
    grad_gain_two = jnp.sum(grad_hidden_two * normed_two, axis=0)
    grad_shift_two = jnp.sum(grad_hidden_two, axis=0)
    grad_residual_one = grad_out + norm_backward(grad_hidden_two, normed_two, inv_two, gain_two)
    grad_scale_one = jnp.sum(grad_residual_one * branch, axis=0)
    grad_branch = (grad_residual_one * scale_one).astype(jnp.bfloat16)
    grad_bias_out = jnp.sum(grad_branch.astype(jnp.float32), axis=0)
    grad_wout = contract_rows(attended, grad_branch)
    grad_attended = contract_cols(grad_branch, out_back).astype(jnp.bfloat16)
    grad_attn_heads = grad_attended.reshape(row_count, head_count, HEAD_DIM)
    row_delta = jnp.sum(grad_attn_heads.astype(jnp.float32) * attn_heads, axis=-1, keepdims=True)
    back_keys, back_values, back_mask = (
        lax.all_gather(key_rows, "context", axis=0, tiled=True),
        lax.all_gather(values, "context", axis=0, tiled=True),
        lax.all_gather(key_mask, "context", axis=0, tiled=True),
    )
    key_count = back_keys.shape[0]
    grad_query = jnp.zeros((row_count, head_count, HEAD_DIM), jnp.float32)
    key_terms = []
    value_terms = []
    for offset in range(0, key_count, 512):
        finish = min(key_count, offset + 512)
        key_block = back_keys[offset:finish].reshape(finish - offset, head_count, HEAD_DIM)
        value_block = back_values[offset:finish].reshape(finish - offset, head_count, HEAD_DIM)
        mask_block = back_mask[offset:finish][None, None, :] > 0
        scores = jnp.einsum(
            "rhe,nhe->rhn", query_heads, key_block, preferred_element_type=jnp.float32
        ) * HEAD_DIM ** (-0.5)
        attn_prob = jnp.where(mask_block, jnp.exp(scores - log_total), 0.0)
        value_terms.append(
            jnp.einsum(
                "rhn,rhe->nhe",
                attn_prob.astype(jnp.bfloat16),
                grad_attn_heads,
                preferred_element_type=jnp.float32,
            )
        )
        grad_prob = jnp.einsum(
            "rhe,nhe->rhn", grad_attn_heads, value_block, preferred_element_type=jnp.float32
        )
        grad_scores = (attn_prob * (grad_prob - row_delta)).astype(jnp.bfloat16)
        grad_query = grad_query + jnp.einsum(
            "rhn,nhe->rhe", grad_scores, key_block, preferred_element_type=jnp.float32
        ) * HEAD_DIM ** (-0.5)
        key_terms.append(
            jnp.einsum("rhn,rhe->nhe", grad_scores, query_heads, preferred_element_type=jnp.float32)
            * HEAD_DIM ** (-0.5)
        )
    key_sums = jnp.concatenate(key_terms, axis=0).reshape(key_count, local_width)
    value_sums = jnp.concatenate(value_terms, axis=0).reshape(key_count, local_width)
    grad_keys, grad_values = (
        lax.psum_scatter(
            key_sums.astype(jnp.bfloat16), "context", scatter_dimension=0, tiled=True
        ).astype(jnp.float32),
        lax.psum_scatter(
            value_sums.astype(jnp.bfloat16), "context", scatter_dimension=0, tiled=True
        ).astype(jnp.float32),
    )
    grad_projected = jnp.stack(
        [grad_query.reshape(row_count, local_width), grad_keys, grad_values], axis=1
    ).astype(jnp.bfloat16)
    grad_float = grad_projected.astype(jnp.float32)
    grad_qv = jnp.stack(
        [jnp.sum(grad_float[:, 0], axis=0), jnp.sum(grad_float[:, 2], axis=0)], axis=0
    )
    grad_flat = grad_projected.reshape(row_count, 3 * local_width)
    grad_qkv = contract_rows(hidden_one, grad_flat).reshape(model_width, 3, local_width)
    grad_hidden_one = lax.psum(
        contract_cols(grad_flat, qkv_back.reshape(model_width, 3 * local_width)).astype(
            jnp.bfloat16
        ),
        "tensor",
    ).astype(jnp.float32)
    grad_gain_one = jnp.sum(grad_hidden_one * normed_one, axis=0)
    grad_shift_one = jnp.sum(grad_hidden_one, axis=0)
    token_grad = grad_residual_one + norm_backward(grad_hidden_one, normed_one, inv_one, gain_one)
    shards = (
        lax.psum_scatter(grad_gain_one, ("dp", "context"), scatter_dimension=0, tiled=True),
        lax.psum_scatter(grad_shift_one, ("dp", "context"), scatter_dimension=0, tiled=True),
        lax.psum_scatter(grad_qkv, ("dp", "context"), scatter_dimension=0, tiled=True),
        lax.psum_scatter(grad_qv, ("dp", "context"), scatter_dimension=1, tiled=True),
        lax.psum_scatter(grad_wout, ("dp", "context"), scatter_dimension=1, tiled=True),
        lax.psum_scatter(grad_bias_out, ("dp", "context"), scatter_dimension=0, tiled=True),
        lax.psum_scatter(grad_scale_one, ("dp", "context"), scatter_dimension=0, tiled=True),
        lax.psum_scatter(grad_gain_two, ("dp", "context"), scatter_dimension=0, tiled=True),
        lax.psum_scatter(grad_shift_two, ("dp", "context"), scatter_dimension=0, tiled=True),
        lax.psum_scatter(grad_fc1, ("dp", "context"), scatter_dimension=0, tiled=True),
        lax.psum_scatter(grad_bias_fc1, ("dp", "context"), scatter_dimension=0, tiled=True),
        lax.psum_scatter(grad_fc2, ("dp", "context"), scatter_dimension=1, tiled=True),
        lax.psum_scatter(grad_bias_fc2, ("dp", "context"), scatter_dimension=0, tiled=True),
        lax.psum_scatter(grad_scale_two, ("dp", "context"), scatter_dimension=0, tiled=True),
    )
    return (block_out[None], token_grad[None]) + tuple(shards)


def solution(mesh):
    return jax.shard_map(
        on_device,
        mesh=mesh,
        in_specs=(
            P("dp", "context", None),
            P("dp", "context"),
            P(("dp", "context")),
            P(("dp", "context")),
            P(("dp", "context"), None, "tensor"),
            P(None, ("tensor", "dp", "context")),
            P("tensor", ("dp", "context")),
            P(("dp", "context")),
            P(("dp", "context")),
            P(("dp", "context")),
            P(("dp", "context")),
            P(("dp", "context"), "tensor"),
            P(("tensor", "dp", "context")),
            P("tensor", ("dp", "context")),
            P(("dp", "context")),
            P(("dp", "context")),
            P("dp", "context", None),
        ),
        out_specs=(
            P("dp", "context", None),
            P("dp", "context", None),
            P(("dp", "context")),
            P(("dp", "context")),
            P(("dp", "context"), None, "tensor"),
            P(None, ("tensor", "dp", "context")),
            P("tensor", ("dp", "context")),
            P(("dp", "context")),
            P(("dp", "context")),
            P(("dp", "context")),
            P(("dp", "context")),
            P(("dp", "context"), "tensor"),
            P(("tensor", "dp", "context")),
            P("tensor", ("dp", "context")),
            P(("dp", "context")),
            P(("dp", "context")),
        ),
        check_vma=False,
    )
```

profile of v0, /device:TPU:16, one launch (start us, length us, event | category | flops | bytes accessed | tf_op | source)
XLA Modules:
  0.0 809.7 jit_solution(9476761996251967744)
XLA Ops:
  8.7 15.3 %all-gather.3 = bf16[8,1,128]{2,1,0:T(2,128)(2,1)S(1)} all-gather(bf16[1,1,128]{2,1,0:T(2,128)(2,1)} %bitcast.338), channel_id=1, replica_groups=mesh['dp'=4,'context'=2,'tensor'=4] {'dp','context'}, dimensions={0}, use_global_device_ids=true | all-gather | bytes 2304 | tf_op jit(solution)/shard_map/all_gather | solution.py:88
  24.0 16.9 %all-gather.4 = bf16[8,1,128]{2,1,0:T(2,128)(2,1)S(1)} all-gather(bf16[1,1,128]{2,1,0:T(2,128)(2,1)} %bitcast.339), channel_id=1, replica_groups=mesh['dp'=4,'context'=2,'tensor'=4] {'dp','context'}, dimensions={0}, use_global_device_ids=true | all-gather | bytes 2304 | tf_op jit(solution)/shard_map/all_gather | solution.py:89
  40.9 18.5 %all-gather.5 = bf16[8,32,2]{1,2,0:T(2,128)(2,1)S(1)} all-gather(bf16[1,32,2]{1,2,0:T(2,128)(2,1)} %bitcast.340), channel_id=1, replica_groups=mesh['dp'=4,'context'=2,'tensor'=4] {'dp','context'}, dimensions={0}, use_global_device_ids=true | all-gather | bytes 1152 | tf_op jit(solution)/shard_map/all_gather | solution.py:91
  59.6 4.3 all-gather
  65.4 1.6 fusion.31
  67.1 30.4 %all_gather.66 = bf16[256,1024]{1,0:T(8,128)(2,1)S(1)} all-gather(bf16[256,128]{1,0:T(8,128)(2,1)S(1)} %copy-done.29), channel_id=1, replica_groups=mesh['dp'=4,'context'=2,'tensor'=4] {'dp','context'}, dimensions={1}, use_global_device_ids=true | all-gather | bytes 589824 | tf_op jit(solution)/shard_map/all_gather | solution.py:92
  97.5 1.9 copy.75
  100.8 7.0 all_gather.65
  107.9 7.1 all-gather.1
  117.3 2.6 fusion.12
  121.1 1.9 fusion.131
  125.9 13.0 %all-gather.6 = bf16[8,1,128]{2,1,0:T(2,128)(2,1)S(1)} all-gather(bf16[1,1,128]{2,1,0:T(2,128)(2,1)S(1)} %bitcast.341), channel_id=1, replica_groups=mesh['dp'=4,'context'=2,'tensor'=4] {'dp','context'}, dimensions={0}, use_global_device_ids=true | all-gather | bytes 2304 | tf_op jit(solution)/shard_map/all_gather | solution.py:93
  138.9 18.1 %all-gather.2 = bf16[8,1,128]{2,1,0:T(2,128)(2,1)S(1)} all-gather(bf16[1,1,128]{2,1,0:T(2,128)(2,1)S(1)} %bitcast.342), channel_id=1, replica_groups=mesh['dp'=4,'context'=2,'tensor'=4] {'dp','context'}, dimensions={0}, use_global_device_ids=true | all-gather | bytes 2304 | tf_op jit(solution)/shard_map/all_gather | solution.py:94
  157.0 16.6 %all-gather.8 = bf16[8,1,128]{2,1,0:T(2,128)(2,1)S(1)} all-gather(bf16[1,1,128]{2,1,0:T(2,128)(2,1)S(1)} %bitcast.343), channel_id=1, replica_groups=mesh['dp'=4,'context'=2,'tensor'=4] {'dp','context'}, dimensions={0}, use_global_device_ids=true | all-gather | bytes 2304 | tf_op jit(solution)/shard_map/all_gather | solution.py:95
  173.7 17.9 %all-gather.9 = bf16[8,1,128]{2,1,0:T(2,128)(2,1)S(1)} all-gather(bf16[1,1,128]{2,1,0:T(2,128)(2,1)S(1)} %bitcast.344), channel_id=1, replica_groups=mesh['dp'=4,'context'=2,'tensor'=4] {'dp','context'}, dimensions={0}, use_global_device_ids=true | all-gather | bytes 2304 | tf_op jit(solution)/shard_map/all_gather | solution.py:96
  191.6 16.8 %all-gather.10 = bf16[8,1,128]{2,1,0:T(2,128)(2,1)S(1)} all-gather(bf16[1,1,128]{2,1,0:T(2,128)(2,1)S(1)} %bitcast.345), channel_id=1, replica_groups=mesh['dp'=4,'context'=2,'tensor'=4] {'dp','context'}, dimensions={0}, use_global_device_ids=true | all-gather | bytes 2304 | tf_op jit(solution)/shard_map/all_gather | solution.py:98
  208.3 17.9 %all-gather.7 = bf16[8,1,128]{2,1,0:T(2,128)(2,1)S(1)} all-gather(bf16[1,1,128]{2,1,0:T(2,128)(2,1)S(1)} %bitcast.346), channel_id=1, replica_groups=mesh['dp'=4,'context'=2,'tensor'=4] {'dp','context'}, dimensions={0}, use_global_device_ids=true | all-gather | bytes 2304 | tf_op jit(solution)/shard_map/all_gather | solution.py:101
  226.2 1.8 fusion.122
  228.7 9.2 %multiply_convert_fusion.1 = (bf16[512,1024]{1,0:T(8,128)(2,1)}, f32[512,1024]{1,0:T(8,128)}, f32[512,1024]{1,0:T(8,128)}) fusion(f32[1024]{0:T(1024)S(1)} %bitcast.334, bf16[1024,1024]{1,0:T(8,128)(2,1)} %all-gather.18.cloned.1.call-done, f32[1024]{0:T(1024)S(1)} %bitcast.332, f32[1024]{0:T(1024)S(1)} %bitcast.322, f32[512]{0:T(512)S(1)} %add_rsqrt_fusion, ...), kind=kOutput, calls=%fused_computation.75 | convolution fusion | flops 1113587712 | bytes 9461760 | tf_op jit(solution)/shard_map/dot_general | solution.py:171
  237.9 25.1 %all-gather.20.cloned.1.call-done = bf16[1024,1024]{1,0:T(8,128)(2,1)} async-done(((bf16[1024,128]{1,0:T(8,128)(2,1)}), bf16[1024,1024]{1,0:T(8,128)(2,1)}) %all-gather.20.cloned.1.call-update) | async-done | bytes 2097168 | tf_op jit(solution)/shard_map/all_gather | solution.py:99
  263.0 4.9 convert_reduce_fusion.4
  268.9 2.3 convolution_convert_fusion
  271.4 35.0 %all-reduce.17.cloned.1.call-done = bf16[512,1024]{1,0:T(8,128)(2,1)} async-done(((bf16[512,1024]{1,0:T(8,128)(2,1)}), bf16[512,1024]{1,0:T(8,128)(2,1)}) %all-reduce.17.cloned.1.call-update) | async-done | bytes 1048592 | tf_op jit(solution)/shard_map/psum | solution.py:198
  306.5 2.6 fusion.41
  317.3 2.8 fusion.3
  320.9 2.0 copy.86
  323.1 2.4 fusion.89
  325.5 3.6 fusion.1
  332.1 2.0 copy.83
  334.2 4.3 convolution_convert_fusion.1
  342.5 12.5 %reduce-scatter.10.cloned.1.call-done = bf16[512,256]{1,0:T(8,128)(2,1)} async-done(((bf16[1024,256]{1,0:T(8,128)(2,1)}), bf16[512,256]{1,0:T(8,128)(2,1)}) %reduce-scatter.10.cloned.1.call-update) | async-done | bytes 262160 | tf_op jit(solution)/shard_map/reduce_scatter | solution.py:251
  355.0 2.1 fusion.127
  358.0 3.6 bitcast_convert_fusion
  362.6 2.6 fusion.133
  365.6 2.3 copy.88
  367.9 4.1 fusion.107
  372.1 4.7 fusion.125
  376.9 4.5 fusion.101
  382.0 14.0 %all-gather.11 = bf16[8,1,128]{2,1,0:T(2,128)(2,1)S(1)} all-gather(bf16[1,1,128]{2,1,0:T(2,128)(2,1)S(1)} %bitcast.347), channel_id=1, replica_groups=mesh['dp'=4,'context'=2,'tensor'=4] {'dp','context'}, dimensions={0}, use_global_device_ids=true | all-gather | bytes 2304 | tf_op jit(solution)/shard_map/all_gather | solution.py:100
  397.3 21.0 %reduce-scatter.22.cloned.1.call-done = f32[32,2]{1,0:T(8,128)} async-done(((f32[256,2]{1,0:T(8,128)}), f32[32,2]{1,0:T(8,128)}) %reduce-scatter.22.cloned.1.call-update) | async-done | bytes 272
  419.6 53.2 %all-reduce.19.cloned.1.call-done = (bf16[512,1024]{1,0:T(8,128)(2,1)}, bf16[512,1024]{1,0:T(8,128)(2,1)}) async-done(((bf16[512,1024]{1,0:T(8,128)(2,1)}, bf16[512,1024]{1,0:T(8,128)(2,1)}), (bf16[512,1024]{1,0:T(8,128)(2,1)}, bf16[512,1024]{1,0:T(8,128)(2,1)})) %all-reduce.19.cloned.1.call-update) | async-done | bytes 2097168 | tf_op jit(solution)/shard_map/psum | solution.py:175
  472.8 2.4 fusion.42
  475.2 4.4 fusion.44
  479.7 33.0 %all-reduce.9 = (f32[1024]{0:T(1024)S(1)}, f32[1024]{0:T(1024)S(1)}, f32[1024]{0:T(1024)S(1)}, f32[1024]{0:T(1024)S(1)}, f32[1024]{0:T(1024)S(1)}, /*index=5*/f3...) all-reduce(f32[1024]{0:T(1024)S(1)} %get-tuple-element.18, ...), channel_id=6, replica_groups=mesh['dp'=4,'context'=2,'tensor'=4] {'dp','context'}, use_global_device_ids=true, to_apply=%region_20.21.clone | all-reduce | flops 9216 | bytes 73728
  518.0 22.2 %reduce-scatter.16.cloned.1.call-done = f32[256,128]{1,0:T(8,128)} async-done(((f32[256,1024]{1,0:T(8,128)}), f32[256,128]{1,0:T(8,128)}) %reduce-scatter.16.cloned.1.call-update) | async-done | bytes 131088 | tf_op jit(solution)/shard_map/reduce_scatter | solution.py:281
  540.1 78.2 %reduce-scatter.14.cloned.1.call-done = f32[128,3,256]{2,0,1:T(8,128)} async-done(((f32[1024,3,256]{2,0,1:T(8,128)}), f32[128,3,256]{2,0,1:T(8,128)}) %reduce-scatter.14.cloned.1.call-update) | async-done | bytes 393232 | tf_op jit(solution)/shard_map/reduce_scatter | solution.py:279
  618.3 91.8 %reduce-scatter.18.cloned.1.call-done = f32[128,1024]{1,0:T(8,128)} async-done(((f32[1024,1024]{1,0:T(8,128)}), f32[128,1024]{1,0:T(8,128)}) %reduce-scatter.18.cloned.1.call-update) | async-done | bytes 524304 | tf_op jit(solution)/shard_map/reduce_scatter | solution.py:286
  710.1 92.7 %reduce-scatter.20.cloned.1.call-done = f32[1024,128]{1,0:T(8,128)} async-done(((f32[1024,1024]{1,0:T(8,128)}), f32[1024,128]{1,0:T(8,128)}) %reduce-scatter.20.cloned.1.call-update) | async-done | bytes 524304 | tf_op jit(solution)/shard_map/reduce_scatter | solution.py:288
  (173 shorter events, 38.8 us)
Async XLA Ops:
  7.2 59.9 %copy-start.29 = (bf16[256,128]{1,0:T(8,128)(2,1)S(1)}, bf16[256,128]{1,0:T(8,128)(2,1)}, u32[]{:S(2)}) copy-start(bf16[256,128]{1,0:T(8,128)(2,1)} %param.23) | copy-start | bytes 196612
  7.2 90.4 %all-gather.16.cloned.1.call-start = ((), (), s32[]{:S(2)}) async-start(), calls=%async_computation.7 | async-start | bytes 1769472 | tf_op jit(solution)/shard_map/all_gather | solution.py:90
  7.9 218.3 %all-reduce.15.cloned.1.call-start = ((), (), s32[]{:S(2)}) async-start(), calls=%async_computation.8 | async-start | bytes 2097152 | tf_op jit(solution)/shard_map/psum | solution.py:162
  67.1 32.4 %copy-start = (bf16[1,512,1024]{2,1,0:T(8,128)(2,1)S(1)}, bf16[1,512,1024]{2,1,0:T(8,128)(2,1)}, u32[]{:S(2)}) copy-start(bf16[1,512,1024]{2,1,0:T(8,128)(2,1)} %param.17) | copy-start | bytes 3145732
  97.5 25.6 %copy-start.13 = (bf16[256,1024]{1,0:T(8,128)(2,1)}, bf16[256,1024]{1,0:T(8,128)(2,1)S(1)}, u32[]{:S(2)}) copy-start(bf16[256,1024]{1,0:T(8,128)(2,1)S(1)} %all_gather.66) | copy-start | bytes 1572868
  107.9 12.0 %copy-start.27 = (bf16[512,256]{0,1:T(8,128)(2,1)}, bf16[512,256]{0,1:T(8,128)(2,1)S(1)}, u32[]{:S(2)}) copy-start(bf16[512,256]{0,1:T(8,128)(2,1)S(1)} %get-tuple-element.55) | copy-start | bytes 786436
  107.9 13.2 %copy-start.25 = (bf16[512,256]{0,1:T(8,128)(2,1)}, bf16[512,256]{0,1:T(8,128)(2,1)S(1)}, u32[]{:S(2)}) copy-start(bf16[512,256]{0,1:T(8,128)(2,1)S(1)} %get-tuple-element.54) | copy-start | bytes 786436
  115.1 1.2 copy-start.16
  116.2 3.7 copy-start.6
  117.3 3.8 copy-start.4
  123.1 103.1 %copy-start.20 = (bf16[512,4,64]{0,2,1:T(8,128)(2,1)}, bf16[512,4,64]{0,2,1:T(8,128)(2,1)S(1)}, u32[]{:S(2)}) copy-start(bf16[512,4,64]{0,2,1:T(8,128)(2,1)S(1)} %get-tuple-element.67) | copy-start | bytes 786436
  123.1 2.9 copy-start.30
  123.1 15.8 %copy-start.31 = (bf16[128]{0:T(256)(128)(2,1)S(1)}, bf16[128]{0:T(256)(128)(2,1)}, u32[]{:S(2)}) copy-start(bf16[128]{0:T(256)(128)(2,1)} %param.25) | copy-start | bytes 772
  123.1 34.0 %copy-start.32 = (bf16[128]{0:T(256)(128)(2,1)S(1)}, bf16[128]{0:T(256)(128)(2,1)}, u32[]{:S(2)}) copy-start(bf16[128]{0:T(256)(128)(2,1)} %param.26) | copy-start | bytes 772
  123.1 50.6 %copy-start.33 = (bf16[128]{0:T(256)(128)(2,1)S(1)}, bf16[128]{0:T(256)(128)(2,1)}, u32[]{:S(2)}) copy-start(bf16[128]{0:T(256)(128)(2,1)} %param.27) | copy-start | bytes 772
  123.1 68.5 %copy-start.34 = (bf16[128]{0:T(256)(128)(2,1)S(1)}, bf16[128]{0:T(256)(128)(2,1)}, u32[]{:S(2)}) copy-start(bf16[128]{0:T(256)(128)(2,1)} %param.29) | copy-start | bytes 772
  123.1 85.2 %copy-start.35 = (bf16[128]{0:T(256)(128)(2,1)S(1)}, bf16[128]{0:T(256)(128)(2,1)}, u32[]{:S(2)}) copy-start(bf16[128]{0:T(256)(128)(2,1)} %param.32) | copy-start | bytes 772
  124.6 104.1 %all-gather.18.cloned.1.call-start = ((), (), s32[]{:S(2)}) async-start(), calls=%async_computation.9 | async-start | bytes 2359296 | tf_op jit(solution)/shard_map/all_gather | solution.py:97
  125.3 137.7 %all-gather.20.cloned.1.call-start = ((), (), s32[]{:S(2)}) async-start(), calls=%async_computation.10 | async-start | bytes 2359296 | tf_op jit(solution)/shard_map/all_gather | solution.py:99
  125.9 180.6 %all-reduce.17.cloned.1.call-start = ((), (), s32[]{:S(2)}) async-start(), calls=%async_computation.11 | async-start | bytes 2097152 | tf_op jit(solution)/shard_map/psum | solution.py:198
  226.2 1.8 copy-start.1
  228.7 34.3 %copy-start.8 = (bf16[1,512,1024]{2,1,0:T(8,128)(2,1)S(1)}, bf16[1,512,1024]{2,1,0:T(8,128)(2,1)}, u32[]{:S(2)}) copy-start(bf16[1,512,1024]{2,1,0:T(8,128)(2,1)} %param.33) | copy-start | bytes 3145732
  263.0 5.9 copy-start.37
  271.2 71.3 %reduce-scatter.12.cloned.1.call-start = ((), (), s32[]{:S(2)}) async-start(), calls=%async_computation.13 | async-start | bytes 786432 | tf_op jit(solution)/shard_map/reduce_scatter | solution.py:254
  306.4 2.6 copy-start.15
  310.4 2.5 copy-start.2
  310.4 1.4 copy-start.14
  310.4 2.0 copy-start.22
  310.4 3.7 copy-start.7
  310.8 2.1 copy-start.9
  312.9 4.4 copy-start.23
  314.1 2.2 copy-start.5
  323.0 32.0 %reduce-scatter.10.cloned.1.call-start = ((), (), s32[]{:S(2)}) async-start(), calls=%async_computation.12 | async-start | bytes 786432 | tf_op jit(solution)/shard_map/reduce_scatter | solution.py:251
  323.1 2.4 copy-start.24
  323.1 2.4 copy-start.26
  329.1 1.4 copy-start.10
  334.2 84.1 %reduce-scatter.22.cloned.1.call-start = ((), (), s32[]{:S(2)}) async-start(), calls=%async_computation.18 | async-start | bytes 147456
  334.2 4.4 copy-start.12
  334.2 4.3 copy-start.19
  338.6 1.6 copy-start.11
  338.6 1.6 copy-start.17
  358.0 114.9 %all-reduce.19.cloned.1.call-start = ((), (), s32[]{:S(2)}) async-start(), calls=%async_computation.19 | async-start | bytes 4194304 | tf_op jit(solution)/shard_map/psum | solution.py:175
  361.7 178.4 %reduce-scatter.16.cloned.1.call-start = ((), (), s32[]{:S(2)}) async-start(), calls=%async_computation.15 | async-start | bytes 1179648 | tf_op jit(solution)/shard_map/reduce_scatter | solution.py:281
  365.3 253.0 %reduce-scatter.14.cloned.1.call-start = ((), (), s32[]{:S(2)}) async-start(), calls=%async_computation.14 | async-start | bytes 3538944 | tf_op jit(solution)/shard_map/reduce_scatter | solution.py:279
  372.0 338.0 %reduce-scatter.18.cloned.1.call-start = ((), (), s32[]{:S(2)}) async-start(), calls=%async_computation.16 | async-start | bytes 4718592 | tf_op jit(solution)/shard_map/reduce_scatter | solution.py:286
  376.8 426.0 %reduce-scatter.20.cloned.1.call-start = ((), (), s32[]{:S(2)}) async-start(), calls=%async_computation.17 | async-start | bytes 4718592 | tf_op jit(solution)/shard_map/reduce_scatter | solution.py:288
  381.4 14.7 %copy-start.38 = (u32[32]{0:T(128)S(1)}, u32[32]{0:T(128)}, u32[]{:S(2)}) copy-start(u32[32]{0:T(128)} %constant.92) | copy-start | bytes 388
  472.8 2.4 copy-start.3
  (5 other events, 4.7 us)
Sparse Core Ops, SparseCore 0:
  10.2 45.0 all-gather.15
  124.7 35.1 all-reduce.14
  162.3 49.2 all-gather.17
  213.7 49.2 all-gather.19
  271.3 35.0 all-reduce.16
  323.1 14.9 reduce-scatter.11
  340.4 14.5 reduce-scatter.9
  358.3 59.8 reduce-scatter.21
  421.3 51.5 all-reduce.18
  477.0 63.0 reduce-scatter.15
  544.3 73.9 reduce-scatter.13
  622.4 87.6 reduce-scatter.17
  714.7 88.0 reduce-scatter.19
where the time goes:
time: 820 us; the launch traced here: 810 us
  waiting for transfers between devices  434 us (53%)
  blocking collectives  247 us (30%)
  matrix products  61.6 us (8%)
  local copies, waits for them, and re-layouts  26.9 us (3%)
  other arithmetic  24.1 us (3%)
  between operations  15.6 us (2%)
    reduce_scatter x1, waiting for transfers between devices, on_device(): lax.psum_scatter(grad_fc2, ('dp', 'context'), scatter_dimension=1, tiled=...  92.7 us
    reduce_scatter x1, waiting for transfers between devices, on_device(): lax.psum_scatter(grad_fc1, ('dp', 'context'), scatter_dimension=0, tiled=...  91.8 us
    reduce_scatter x1, waiting for transfers between devices, on_device(): lax.psum_scatter(grad_qkv, ('dp', 'context'), scatter_dimension=0, tiled=...  78.2 us
    psum x1, waiting for transfers between devices, on_device(): lax.psum(jnp.dot(hidden, fc2_full, preferred_element_type=jnp.float32).as...  53.2 us
    psum x1, waiting for transfers between devices, on_device(): lax.psum(contract_cols(grad_pre, fc1_back).astype(jnp.bfloat16), 'tensor')  35 us
    unnamed x1, blocking collectives  33 us
    all_gather x1, blocking collectives, on_device(): lax.all_gather(w_out, ('dp', 'context'), axis=1, tiled=True)  30.4 us
    all_gather x1, waiting for transfers between devices, on_device(): lax.all_gather(w_fc2, ('dp', 'context'), axis=1, tiled=True)  25.1 us
  transfers between devices with their start and end apart: 13, of which 9 were waited for; matrix products, arithmetic and copies ran while one was open for 8% of the time, Pallas kernels for 0%

commit v1 on v0

--- a/solution.py
+++ b/solution.py
@@ -1,10 +1,16 @@
+import functools
+import math
+
 import jax
 import jax.numpy as jnp
 from jax import lax
+from jax.experimental import pallas as pl
+from jax.experimental.pallas import tpu as pltpu
 from jax.sharding import PartitionSpec as P
 
 HEAD_DIM = 64
-
+MESH = pl.DeviceIdType.MESH
+VMEM_LIMIT = 56 * 1024 * 1024
 
 EPSILON = 1e-06
 NEGATIVE = -1e30
@@ -64,6 +70,436 @@
         running_max = new_max
     return (running_max, running_total, running_sum)
 
+
+def params(ident):
+    return pltpu.CompilerParams(
+        collective_id=ident, has_side_effects=True, vmem_limit_bytes=VMEM_LIMIT
+    )
+
+
+def greet(count, device_id):
+    pl.semaphore_signal(
+        pltpu.get_barrier_semaphore(), inc=count, device_id=device_id, device_id_type=MESH
+    )
+
+
+def remote(src, dst, send_sem, recv_sem, device_id):
+    return pltpu.make_async_remote_copy(
+        src_ref=src,
+        dst_ref=dst,
+        send_sem=send_sem,
+        recv_sem=recv_sem,
+        device_id=device_id,
+        device_id_type=MESH,
+    )
+
+
+def greet_line(line):
+    here = lax.axis_index("dp")
+    side = lax.axis_index("context")
+    greet(1, {"context": 1 - side})
+
+    @pl.when(here < line - 1)
+    def _():
+        greet(1, {"dp": here + 1})
+
+    @pl.when(here > 0)
+    def _():
+        greet(1, {"dp": here - 1})
+
+    above = jnp.where(here < line - 1, 1, 0)
+    below = jnp.where(here > 0, 1, 0)
+    pl.semaphore_wait(pltpu.get_barrier_semaphore(), 1 + above + below)
+
+
+def owner_view(ref, owner, width):
+    if len(ref.shape) == 3:
+        return ref.at[owner]
+    return ref.at[:, pl.ds(pl.multiple_of(owner * width, width), width)]
+
+
+def gather_kernel(line, count, *refs):
+    ins, outs = refs[:count], refs[count : 2 * count]
+    send, recv, local = refs[2 * count :]
+    here = lax.axis_index("dp")
+    side = lax.axis_index("context")
+    cross = 2 * (line - 1)
+
+    def part(a, row, column):
+        return owner_view(outs[a], row * 2 + column, ins[a].shape[-1])
+
+    def up(a, s, row):
+        src = ins[a] if s == 0 else part(a, row, side)
+        return remote(
+            src, part(a, row, side), send.at[a, s], recv.at[a, s], {"dp": here + 1}
+        )
+
+    def down(a, s, row):
+        src = ins[a] if s == 0 else part(a, row, side)
+        slot = line - 1 + s
+        return remote(
+            src, part(a, row, side), send.at[a, slot], recv.at[a, slot], {"dp": here - 1}
+        )
+
+    def over(a, row, own):
+        src = ins[a] if own else part(a, row, side)
+        return remote(
+            src,
+            part(a, row, side),
+            send.at[a, cross + row],
+            recv.at[a, cross + row],
+            {"context": 1 - side},
+        )
+
+    greet_line(line)
+    for a in range(count):
+
+        @pl.when(here < line - 1)
+        def _():
+            up(a, 0, here).start()
+
+        @pl.when(here > 0)
+        def _():
+            down(a, 0, here).start()
+
+        over(a, here, True).start()
+        pltpu.make_async_copy(ins[a], part(a, here, side), local.at[a]).start()
+    for s in range(1, line):
+        for a in range(count):
+
+            @pl.when(here - s >= 0)
+            def _():
+                up(a, s - 1, here - s).wait_recv()
+
+                @pl.when(here < line - 1)
+                def _():
+                    up(a, s, here - s).start()
+
+                over(a, here - s, False).start()
+
+            @pl.when(here + s <= line - 1)
+            def _():
+                down(a, s - 1, here + s).wait_recv()
+
+                @pl.when(here > 0)
+                def _():
+                    down(a, s, here + s).start()
+
+                over(a, here + s, False).start()
+
+    for a in range(count):
+        pltpu.make_async_copy(ins[a], part(a, here, side), local.at[a]).wait()
+        for row in range(line):
+            remote(
+                part(a, row, 1 - side),
+                part(a, row, 1 - side),
+                send.at[a, cross + row],
+                recv.at[a, cross + row],
+                {"context": 1 - side},
+            ).wait_recv()
+            over(a, row, False).wait_send()
+        for s in range(line - 1):
+
+            @pl.when((here < line - 1) & (here - s >= 0))
+            def _():
+                up(a, s, here - s).wait_send()
+
+            @pl.when((here > 0) & (here + s <= line - 1))
+            def _():
+                down(a, s, here + s).wait_send()
+
+
+def gather_parts(arrays, stacked, line, ident):
+    owners = line * 2
+    shapes = []
+    for array, stack in zip(arrays, stacked):
+        if stack:
+            shape = (owners,) + array.shape
+        else:
+            shape = (array.shape[0], owners * array.shape[1])
+        shapes.append(jax.ShapeDtypeStruct(shape, array.dtype))
+    count = len(arrays)
+    slots = 2 * (line - 1) + line
+    return pl.pallas_call(
+        functools.partial(gather_kernel, line, count),
+        out_shape=tuple(shapes),
+        in_specs=[pl.BlockSpec(memory_space=pl.ANY)] * count,
+        out_specs=tuple([pl.BlockSpec(memory_space=pl.ANY)] * count),
+        scratch_shapes=[
+            pltpu.SemaphoreType.DMA((count, slots)),
+            pltpu.SemaphoreType.DMA((count, slots)),
+            pltpu.SemaphoreType.DMA((count,)),
+        ],
+        compiler_params=params(ident),
+    )(*arrays)
+
+
+def swap_kernel(in_ref, out_ref, send, recv):
+    side = lax.axis_index("context")
+    greet(1, {"context": 1 - side})
+    pl.semaphore_wait(pltpu.get_barrier_semaphore(), 1)
+    copy = remote(in_ref, out_ref, send, recv, {"context": 1 - side})
+    copy.start()
+    copy.wait()
+
+
+def swap(array, ident):
+    return pl.pallas_call(
+        swap_kernel,
+        out_shape=jax.ShapeDtypeStruct(array.shape, array.dtype),
+        in_specs=[pl.BlockSpec(memory_space=pl.ANY)],
+        out_specs=pl.BlockSpec(memory_space=pl.ANY),
+        scratch_shapes=[pltpu.SemaphoreType.DMA, pltpu.SemaphoreType.DMA],
+        compiler_params=params(ident),
+    )(array)
+
+
+PIECES = 4
+
+
+def tensor_sum_kernel(count, *refs):
+    ins, outs = refs[:count], refs[count : 2 * count]
+    pair_buf, sum_buf, far_buf, send, recv = refs[2 * count :]
+    place = lax.axis_index("tensor")
+    core = lax.rem(place, 2)
+    pair = {"tensor": place + 1 - 2 * core}
+    far = {"tensor": lax.rem(place + 2, 4)}
+    greet(1, pair)
+    greet(1, far)
+    pl.semaphore_wait(pltpu.get_barrier_semaphore(), 2)
+    half = ins[0].shape[0] // 2
+    step = half // PIECES
+
+    def rows(which, p):
+        return pl.ds(pl.multiple_of(which * half + p * step, step), step)
+
+    def first(a, p):
+        return remote(
+            ins[a].at[rows(1 - core, p)],
+            pair_buf.at[a, p],
+            send.at[0, a, p],
+            recv.at[0, a, p],
+            pair,
+        )
+
+    def second(a, p):
+        return remote(
+            sum_buf.at[a, p], far_buf.at[a, p], send.at[1, a, p], recv.at[1, a, p], far
+        )
+
+    def third(a, p):
+        return remote(
+            outs[a].at[rows(core, p)],
+            outs[a].at[rows(core, p)],
+            send.at[2, a, p],
+            recv.at[2, a, p],
+            pair,
+        )
+
+    todo = [(a, p) for a in range(count) for p in range(PIECES)]
+    for a, p in todo:
+        first(a, p).start()
+    for a, p in todo:
+        first(a, p).wait_recv()
+        total = ins[a][rows(core, p), :].astype(jnp.float32) + pair_buf[a, p].astype(jnp.float32)
+        sum_buf[a, p] = total.astype(jnp.bfloat16)
+        second(a, p).start()
+    for a, p in todo:
+        second(a, p).wait_recv()
+        total = sum_buf[a, p].astype(jnp.float32) + far_buf[a, p].astype(jnp.float32)
+        outs[a][rows(core, p), :] = total.astype(jnp.bfloat16)
+        third(a, p).start()
+    for a, p in todo:
+        remote(
+            outs[a].at[rows(1 - core, p)],
+            outs[a].at[rows(1 - core, p)],
+            send.at[2, a, p],
+            recv.at[2, a, p],
+            pair,
+        ).wait_recv()
+        first(a, p).wait_send()
+        second(a, p).wait_send()
+        third(a, p).wait_send()
+
+
+def tensor_sum(arrays, ident):
+    count = len(arrays)
+    rows, width = arrays[0].shape
+    buf = pltpu.VMEM((count, PIECES, rows // 2 // PIECES, width), jnp.bfloat16)
+    return pl.pallas_call(
+        functools.partial(tensor_sum_kernel, count),
+        out_shape=tuple(jax.ShapeDtypeStruct(a.shape, a.dtype) for a in arrays),
+        in_specs=[pl.BlockSpec(memory_space=pltpu.VMEM)] * count,
+        out_specs=tuple([pl.BlockSpec(memory_space=pltpu.VMEM)] * count),
+        scratch_shapes=[
+            buf,
+            buf,
+            buf,
+            pltpu.SemaphoreType.DMA((3, count, PIECES)),
+            pltpu.SemaphoreType.DMA((3, count, PIECES)),
+        ],
+        compiler_params=params(ident),
+    )(*arrays)
+
+
+def add_rows(dst, terms):
+    count, width = dst.shape
+    block = math.gcd(count, 64 if width > 512 else 256)
+
+    def body(i, carry):
+        at = pl.ds(pl.multiple_of(i * block, block), block)
+        total = terms[0][at, :].astype(jnp.float32)
+        for term in terms[1:]:
+            total = total + term[at, :].astype(jnp.float32)
+        dst[at, :] = total.astype(dst.dtype)
+        return carry
+
+    lax.fori_loop(0, count // block, body, 0)
+
+
+def scatter_kernel(line, count, *refs):
+    ins, outs = refs[:count], refs[count : 2 * count]
+    cross = refs[2 * count : 3 * count]
+    climb = refs[3 * count : 4 * count]
+    fall = refs[4 * count : 5 * count]
+    send, recv = refs[5 * count :]
+    here = lax.axis_index("dp")
+    side = lax.axis_index("context")
+
+    def mine(a, row, column):
+        return owner_view(ins[a], row * 2 + column, outs[a].shape[-1])
+
+    def over(a, row):
+        return remote(
+            mine(a, row, 1 - side),
+            cross[a].at[row],
+            send.at[0, a, row],
+            recv.at[0, a, row],
+            {"context": 1 - side},
+        )
+
+    def up(a, row):
+        return remote(
+            cross[a].at[row],
+            climb[a].at[row],
+            send.at[1, a, row],
+            recv.at[1, a, row],
+            {"dp": here + 1},
+        )
+
+    def down(a, row):
+        return remote(
+            cross[a].at[row],
+            fall[a].at[row],
+            send.at[2, a, row],
+            recv.at[2, a, row],
+            {"dp": here - 1},
+        )
+
+    greet_line(line)
+    for k in range(line // 2):
+        for a in range(count):
+            over(a, line - 1 - k).start()
+            over(a, k).start()
+    for k in range(line - 1):
+        for a in range(count):
+            high, low = line - 1 - k, k
+
+            @pl.when(here < high)
+            def _():
+                over(a, high).wait_recv()
+
+                @pl.when(here == 0)
+                def _():
+                    add_rows(cross[a].at[high], [mine(a, high, side), cross[a].at[high]])
+
+                @pl.when(here > 0)
+                def _():
+                    up(a, high).wait_recv()
+                    add_rows(
+                        cross[a].at[high],
+                        [mine(a, high, side), cross[a].at[high], climb[a].at[high]],
+                    )
+
+                up(a, high).start()
+
+            @pl.when(here > low)
+            def _():
+                over(a, low).wait_recv()
+
+                @pl.when(here == line - 1)
+                def _():
+                    add_rows(cross[a].at[low], [mine(a, low, side), cross[a].at[low]])
+
+                @pl.when(here < line - 1)
+                def _():
+                    down(a, low).wait_recv()
+                    add_rows(
+                        cross[a].at[low],
+                        [mine(a, low, side), cross[a].at[low], fall[a].at[low]],
+                    )
+
+                down(a, low).start()
+
+    for a in range(count):
+        over(a, here).wait_recv()
+        own = [mine(a, here, side), cross[a].at[here]]
+
+        @pl.when(here == 0)
+        def _():
+            down(a, here).wait_recv()
+            add_rows(outs[a], own + [fall[a].at[here]])
+
+        @pl.when(here == line - 1)
+        def _():
+            up(a, here).wait_recv()
+            add_rows(outs[a], own + [climb[a].at[here]])
+
+        @pl.when((here > 0) & (here < line - 1))
+        def _():
+            down(a, here).wait_recv()
+            up(a, here).wait_recv()
+            add_rows(outs[a], own + [climb[a].at[here], fall[a].at[here]])
+
+    for a in range(count):
+        for row in range(line):
+            over(a, row).wait_send()
+
+            @pl.when(here < row)
+            def _():
+                up(a, row).wait_send()
+
+            @pl.when(here > row)
+            def _():
+                down(a, row).wait_send()
+
+
+def scatter_parts(arrays, line, ident):
+    owners = 2 * line
+    count = len(arrays)
+    outs = []
+    for array in arrays:
+        if array.ndim == 3:
+            outs.append(array.shape[1:])
+        else:
+            outs.append((array.shape[0], array.shape[1] // owners))
+    bufs = [pltpu.VMEM((line,) + o, a.dtype) for o, a in zip(outs, arrays)]
+    return pl.pallas_call(
+        functools.partial(scatter_kernel, line, count),
+        out_shape=tuple(jax.ShapeDtypeStruct(o, jnp.float32) for o in outs),
+        in_specs=[pl.BlockSpec(memory_space=pltpu.VMEM)] * count,
+        out_specs=tuple([pl.BlockSpec(memory_space=pltpu.VMEM)] * count),
+        scratch_shapes=bufs * 3
+        + [pltpu.SemaphoreType.DMA((3, count, line)), pltpu.SemaphoreType.DMA((3, count, line))],
+        compiler_params=params(ident),
+    )(*arrays)
+
+
+def pack_rows(vectors, owners, dtype):
+    rows = [v.reshape(owners, -1).astype(dtype) for v in vectors]
+    rows = [jnp.pad(r, ((0, 0), (0, -r.shape[1] % 128))).reshape(owners, -1, 128) for r in rows]
+    packed = jnp.concatenate(rows, axis=1)
+    return jnp.pad(packed, ((0, 0), (0, 16 - packed.shape[1]), (0, 0)))
 
 def on_device(
     tokens,
@@ -292,9 +728,268 @@
     return (block_out[None], token_grad[None]) + tuple(shards)
 
 
+def on_device_line(
+    line,
+    tokens,
+    key_valid,
+    norm1_gain,
+    norm1_shift,
+    w_qkv,
+    qv_bias,
+    w_out,
+    out_bias,
+    scale1,
+    norm2_gain,
+    norm2_shift,
+    w_fc1,
+    fc1_bias,
+    w_fc2,
+    fc2_bias,
+    scale2,
+    cotangent,
+):
+    owners = 2 * line
+    mask_row = key_valid[0].astype(jnp.bfloat16)
+    packed = pack_rows(
+        [
+            norm1_gain,
+            norm1_shift,
+            out_bias,
+            scale1,
+            norm2_gain,
+            norm2_shift,
+            fc2_bias,
+            scale2,
+            fc1_bias,
+            qv_bias,
+            mask_row,
+        ],
+        1,
+        jnp.bfloat16,
+    )[0]
+    pack_full, qkv_full, out_full, fc1_full, fc2_full = gather_parts(
+        [packed, w_qkv.reshape(w_qkv.shape[0], -1), w_out, w_fc1, w_fc2],
+        [True, True, False, True, False],
+        line,
+        1,
+    )
+    qkv_full = qkv_full.reshape((-1,) + w_qkv.shape[1:])
+    fc1_full = fc1_full.reshape(-1, fc1_full.shape[-1])
+    (
+        gain_one,
+        shift_one,
+        bias_out,
+        scale_one,
+        gain_two,
+        shift_two,
+        bias_fc2,
+        scale_two,
+        bias_fc1,
+    ) = [pack_full[:, i].reshape(-1) for i in range(9)]
+    qv_width = qv_bias.shape[1]
+    qv_full = pack_full[:, 9, : 2 * qv_width].reshape(owners, 2, qv_width)
+    qv_full = qv_full.transpose(1, 0, 2).reshape(2, -1)
+    mask_rows = mask_row.shape[0] // 128
+    mask_part = lax.dynamic_slice_in_dim(pack_full, lax.axis_index("dp") * 2, 2, axis=0)
+    full_mask = mask_part[:, 10 : 10 + mask_rows].reshape(-1)
+    side = lax.axis_index("context")
+    gain_one = gain_one.astype(jnp.float32)
+    shift_one = shift_one.astype(jnp.float32)
+    bias_out = bias_out.astype(jnp.float32)
+    scale_one = scale_one.astype(jnp.float32)
+    gain_two = gain_two.astype(jnp.float32)
+    shift_two = shift_two.astype(jnp.float32)
+    bias_fc1 = bias_fc1.astype(jnp.float32)
+    bias_fc2 = bias_fc2.astype(jnp.float32)
+    scale_two = scale_two.astype(jnp.float32)
+    qv_float = qv_full.astype(jnp.float32)
+    residual = tokens[0].astype(jnp.float32)
+    row_count = residual.shape[0]
+    model_width = residual.shape[1]
+    local_width = qkv_full.shape[2]
+    head_count = local_width // HEAD_DIM
+    normed_one, inv_one = normalize(residual)
+    hidden_one = (normed_one * gain_one + shift_one).astype(jnp.bfloat16)
+    projected = jnp.dot(
+        hidden_one,
+        qkv_full.reshape(model_width, 3 * local_width),
+        preferred_element_type=jnp.float32,
+    ).reshape(row_count, 3, local_width)
+    queries = (projected[:, 0] + qv_float[0]).astype(jnp.bfloat16)
+    key_rows = projected[:, 1].astype(jnp.bfloat16)
+    values = (projected[:, 2] + qv_float[1]).astype(jnp.bfloat16)
+    query_heads = queries.reshape(row_count, head_count, HEAD_DIM)
+    key_value = jnp.concatenate([key_rows, values], axis=1)
+    other = swap(key_value, 2)
+    pair = jnp.where(
+        side == 0, jnp.concatenate([key_value, other]), jnp.concatenate([other, key_value])
+    )
+    back_keys, back_values = pair[:, :local_width], pair[:, local_width:]
+    start_carry = (
+        jnp.full((row_count, head_count, 1), NEGATIVE, jnp.float32),
+        jnp.zeros((row_count, head_count, 1), jnp.float32),
+        jnp.zeros((row_count, head_count, HEAD_DIM), jnp.float32),
+    )
+    running_max, running_total, running_sum = attend(
+        start_carry,
+        query_heads,
+        back_keys,
+        back_values,
+        full_mask,
+    )
+    attn_heads = running_sum / running_total
+    log_total = running_max + jnp.log(running_total)
+    attended = attn_heads.reshape(row_count, local_width).astype(jnp.bfloat16)
+    branch = (
+        tensor_sum(
+            [jnp.dot(attended, out_full, preferred_element_type=jnp.float32).astype(jnp.bfloat16)], 4
+        )[0].astype(jnp.float32)
+        + bias_out
+    )
+    residual_one = residual + scale_one * branch
+    normed_two, inv_two = normalize(residual_one)
+    hidden_two = (normed_two * gain_two + shift_two).astype(jnp.bfloat16)
+    pre_act = jnp.dot(hidden_two, fc1_full, preferred_element_type=jnp.float32) + bias_fc1
+    activated, gelu_pull = jax.vjp(lambda value: jax.nn.gelu(value, approximate=False), pre_act)
+    hidden = activated.astype(jnp.bfloat16)
+    mlp_part = jnp.dot(hidden, fc2_full, preferred_element_type=jnp.float32).astype(jnp.bfloat16)
+    grad_out = cotangent[0].astype(jnp.float32)
+    grad_mlp = (grad_out * scale_two).astype(jnp.bfloat16)
+    grad_bias_fc2 = jnp.sum(grad_mlp.astype(jnp.float32), axis=0)
+    grad_fc2 = contract_rows(hidden, grad_mlp)
+    grad_act = contract_cols(grad_mlp, fc2_full)
+    grad_pre = gelu_pull(grad_act)[0].astype(jnp.bfloat16)
+    grad_bias_fc1 = jnp.sum(grad_pre.astype(jnp.float32), axis=0)
+    grad_fc1 = contract_rows(hidden_two, grad_pre)
+    grad_part = contract_cols(grad_pre, fc1_full).astype(jnp.bfloat16)
+    grad_hidden_two, mlp_sum = tensor_sum([grad_part, mlp_part], 5)
+    grad_hidden_two = grad_hidden_two.astype(jnp.float32)
+    mlp_out = mlp_sum.astype(jnp.float32) + bias_fc2
+    block_out = (residual_one + scale_two * mlp_out).astype(jnp.bfloat16)
+    grad_scale_two = jnp.sum(grad_out * mlp_out, axis=0)
+    grad_gain_two = jnp.sum(grad_hidden_two * normed_two, axis=0)
+    grad_shift_two = jnp.sum(grad_hidden_two, axis=0)
+    grad_residual_one = grad_out + norm_backward(grad_hidden_two, normed_two, inv_two, gain_two)
+    grad_scale_one = jnp.sum(grad_residual_one * branch, axis=0)
+    grad_branch = (grad_residual_one * scale_one).astype(jnp.bfloat16)
+    grad_bias_out = jnp.sum(grad_branch.astype(jnp.float32), axis=0)
+    grad_wout = contract_rows(attended, grad_branch)
+    grad_attended = contract_cols(grad_branch, out_full).astype(jnp.bfloat16)
+    grad_attn_heads = grad_attended.reshape(row_count, head_count, HEAD_DIM)
+    row_delta = jnp.sum(grad_attn_heads.astype(jnp.float32) * attn_heads, axis=-1, keepdims=True)
+    back_mask = full_mask
+    key_count = back_keys.shape[0]
+    grad_query = jnp.zeros((row_count, head_count, HEAD_DIM), jnp.float32)
+    key_terms = []
+    value_terms = []
+    for offset in range(0, key_count, 512):
+        finish = min(key_count, offset + 512)
+        key_block = back_keys[offset:finish].reshape(finish - offset, head_count, HEAD_DIM)
+        value_block = back_values[offset:finish].reshape(finish - offset, head_count, HEAD_DIM)
+        mask_block = back_mask[offset:finish][None, None, :] > 0
+        scores = jnp.einsum(
+            "rhe,nhe->rhn", query_heads, key_block, preferred_element_type=jnp.float32
+        ) * HEAD_DIM ** (-0.5)
+        attn_prob = jnp.where(mask_block, jnp.exp(scores - log_total), 0.0)
+        value_terms.append(
+            jnp.einsum(
+                "rhn,rhe->nhe",
+                attn_prob.astype(jnp.bfloat16),
+                grad_attn_heads,
+                preferred_element_type=jnp.float32,
+            )
+        )
+        grad_prob = jnp.einsum(
+            "rhe,nhe->rhn", grad_attn_heads, value_block, preferred_element_type=jnp.float32
+        )
+        grad_scores = (attn_prob * (grad_prob - row_delta)).astype(jnp.bfloat16)
+        grad_query = grad_query + jnp.einsum(
+            "rhn,nhe->rhe", grad_scores, key_block, preferred_element_type=jnp.float32
+        ) * HEAD_DIM ** (-0.5)
+        key_terms.append(
+            jnp.einsum("rhn,rhe->nhe", grad_scores, query_heads, preferred_element_type=jnp.float32)
+            * HEAD_DIM ** (-0.5)
+        )
+    key_sums = jnp.concatenate(key_terms, axis=0).reshape(key_count, local_width)
+    value_sums = jnp.concatenate(value_terms, axis=0).reshape(key_count, local_width)
+    sums = jnp.concatenate([key_sums, value_sums], axis=1)
+    away = lax.dynamic_slice_in_dim(sums, (1 - side) * row_count, row_count, axis=0)
+    home = lax.dynamic_slice_in_dim(sums, side * row_count, row_count, axis=0)
+    home = home + swap(away.astype(jnp.bfloat16), 3).astype(jnp.float32)
+    grad_keys, grad_values = home[:, :local_width], home[:, local_width:]
+    grad_projected = jnp.stack(
+        [grad_query.reshape(row_count, local_width), grad_keys, grad_values], axis=1
+    ).astype(jnp.bfloat16)
+    grad_float = grad_projected.astype(jnp.float32)
+    grad_qv = jnp.stack(
+        [jnp.sum(grad_float[:, 0], axis=0), jnp.sum(grad_float[:, 2], axis=0)], axis=0
+    )
+    grad_flat = grad_projected.reshape(row_count, 3 * local_width)
+    grad_qkv = contract_rows(hidden_one, grad_flat)
+    grad_hidden_one = tensor_sum(
+        [
+            contract_cols(grad_flat, qkv_full.reshape(model_width, 3 * local_width)).astype(
+                jnp.bfloat16
+            )
+        ],
+        6,
+    )[0].astype(jnp.float32)
+    grad_gain_one = jnp.sum(grad_hidden_one * normed_one, axis=0)
+    grad_shift_one = jnp.sum(grad_hidden_one, axis=0)
+    token_grad = grad_residual_one + norm_backward(grad_hidden_one, normed_one, inv_one, gain_one)
+    qv_rows = grad_qv.reshape(2, owners, qv_width).transpose(1, 0, 2)
+    grad_pack = pack_rows(
+        [
+            grad_gain_one,
+            grad_shift_one,
+            grad_bias_out,
+            grad_scale_one,
+            grad_gain_two,
+            grad_shift_two,
+            grad_bias_fc2,
+            grad_scale_two,
+            grad_bias_fc1,
+            qv_rows,
+        ],
+        owners,
+        jnp.float32,
+    )
+    pack_sum, qkv_sum, out_sum, fc1_sum, fc2_sum = scatter_parts(
+        [
+            grad_pack,
+            grad_qkv.astype(jnp.bfloat16).reshape(owners, -1, 3 * local_width),
+            grad_wout.astype(jnp.bfloat16),
+            grad_fc1.astype(jnp.bfloat16).reshape(owners, -1, grad_fc1.shape[1]),
+            grad_fc2.astype(jnp.bfloat16),
+        ],
+        line,
+        7,
+    )
+    return (
+        block_out[None],
+        token_grad[None],
+        pack_sum[0],
+        pack_sum[1],
+        qkv_sum.reshape(w_qkv.shape),
+        pack_sum[9, : 2 * qv_width].reshape(2, qv_width),
+        out_sum,
+        pack_sum[2],
+        pack_sum[3],
+        pack_sum[4],
+        pack_sum[5],
+        fc1_sum,
+        pack_sum[8],
+        fc2_sum,
+        pack_sum[6],
+        pack_sum[7],
+    )
+
+
 def solution(mesh):
+    line = mesh.shape["dp"]
+    own_kernels = mesh.shape["context"] == 2 and mesh.shape["tensor"] == 4 and line == 4
     return jax.shard_map(
-        on_device,
+        functools.partial(on_device_line, line) if own_kernels else on_device,
         mesh=mesh,
         in_specs=(
             P("dp", "context", None),

time: 820 us -> 404 us (0.49); the launches traced: 810 us -> 403 us
  waiting for transfers between devices: 434 us -> 0 us
  Pallas kernels: 0 us -> 268 us
  blocking collectives: 247 us -> 0 us
  between operations: 15.6 us -> 1.53 us
    reduce_scatter x6 -> x0, waiting for transfers between devices: 297 us -> none  [the longest x1 92.7 us: on_device(): lax.psum_scatter(grad_fc2, ('dp', 'context'), scatter_dimension=1, tiled=...]
    pallas_call x0 -> x7, Pallas kernels: none -> 268 us  [the longest x1 99.8 us: scatter_parts(): pl.pallas_call(functools.partial(scatter_kernel, line, count), out_shape=...]
    all_gather x14 -> x0, blocking collectives: 214 us -> none  [the longest x1 30.4 us: on_device(): lax.all_gather(w_out, ('dp', 'context'), axis=1, tiled=True)]
    psum x3 -> x0, waiting for transfers between devices: 88.3 us -> none  [the longest x1 53.2 us: on_device(): lax.psum(jnp.dot(hidden, fc2_full, preferred_element_type=jnp.float32).as...]
    unnamed x1 -> x0, blocking collectives: 33 us -> none
    all_gather x3 -> x0, waiting for transfers between devices: 25.1 us -> none  [the longest x1 25.1 us: on_device(): lax.all_gather(w_fc2, ('dp', 'context'), axis=1, tiled=True)]
    unnamed x14 -> x0, waiting for transfers between devices: 23 us -> none
    dot_general x4, matrix products: 15.9 us -> 24.9 us  [contract_rows(): lax.dot_general(first_matrix, second_matrix, (((0,), (0,)), ((), ())), pr...]
  transfers between devices with their start and end apart: 13 -> 0, of which waited for: 9 -> 0; matrix products, arithmetic and copies ran while one was open for 8% -> 0% of each run, Pallas kernels for 0% -> 0%
where the time goes in v1:
time: 404 us; the launch traced here: 403 us
  Pallas kernels  268 us (66%)
  matrix products  69.2 us (17%)
  other arithmetic  32.2 us (8%)
  local copies, waits for them, and re-layouts  31.8 us (8%)
    pallas_call x1, Pallas kernels, scatter_parts(): pl.pallas_call(functools.partial(scatter_kernel, line, count), out_shape=...  99.8 us
    pallas_call x1, Pallas kernels, gather_parts(): pl.pallas_call(functools.partial(gather_kernel, line, count), out_shape=t...  72.6 us
    pallas_call x3, Pallas kernels, tensor_sum(): pl.pallas_call(functools.partial(tensor_sum_kernel, count), out_shape=tup...  68 us
    pallas_call x2, Pallas kernels, swap(): pl.pallas_call(swap_kernel, out_shape=jax.ShapeDtypeStruct(array.shape, a...  27.7 us
    dot_general x4, matrix products, contract_rows(): lax.dot_general(first_matrix, second_matrix, (((0,), (0,)), ((), ())), pr...  24.9 us
    unnamed x81, local copies, waits for them, and re-layouts  10.1 us
    dot_general x4, matrix products, contract_cols(): lax.dot_general(first_matrix, second_matrix, (((1,), (1,)), ((), ())), pr...  8.45 us

profile of v1, /device:TPU:16, one launch (start us, length us, event | category | flops | bytes accessed | tf_op | source)
XLA Modules:
  0.0 402.8 jit_solution(8914843470205639792)
XLA Ops:
  0.7 1.2 copy.57
  4.1 1.5 concatenate.25
  6.2 72.6 %shard_map.288 = (bf16[8,16,128]{2,1,0:T(8,128)(2,1)}, bf16[8,128,768]{2,1,0:T(8,128)(2,1)}, bf16[256,1024]{1,0:T(8,128)(2,1)}, bf16[8,128,1024]{2,1,0:T(8,128)(2,1)}, bf16[1024,1024]{1,0:T(8,128)(2,1)}) custom-call(bf16[16,128]{1,0:T(8,128)(2,1)} %pad_bitcast_fusion.refs_0_, bf16[128,768]{1,0:T(8,128)(2,1)} %copy.58.refs_1_, bf16[256,128]{1,0:T(8,128)(2,1)} %refs_2_.1, ...), custom_call_target="tpu_custom_call" | custom-call | tf_op jit(solution)/shard_map/pallas_call | solution.py:223
  80.5 1.6 copy.59
  82.1 2.6 fusion.93
  87.1 1.1 slice.162
  89.1 13.1 %shard_map.289 = bf16[512,512]{1,0:T(8,128)(2,1)} custom-call(bf16[512,512]{1,0:T(8,128)(2,1)} %pad_maximum_fusion.3.in_ref), custom_call_target="tpu_custom_call" | custom-call | tf_op jit(solution)/shard_map/pallas_call | solution.py:247
  102.2 1.6 maximum_select_fusion
  104.9 2.9 fusion.9
  109.0 1.9 copy-done.2
  110.9 2.9 fusion.12
  114.0 3.4 fusion.83
  117.6 4.2 %fusion.124 = (bf16[512,4,64]{0,2,1:T(8,128)(2,1)S(1)}, f32[512,4,64]{0,2,1:T(8,128)}) fusion(f32[512,4]{0,1:T(4,128)S(1)} %get-tuple-element.91, f32[512,4,64]{0,2,1:T(8,128)S(1)} %fusion.83, bf16[512,4,64]{0,2,1:T(8,128)(2,1)S(1)} %bitcast.322, f32[4,512,512]{2,1,0:T(8,128)} %get-tuple-element.134, f32[512,4]{0,1:T(4,128)S(1)} %get-tuple-element.129, ...), kind=kOutput, calls=%fused_computation.211 | convolution fusion | flops 139853824 | bytes 5784064 | tf_op jit(solution)/shard_map/rhn,nhe->rhe/dot_general | solution.py:64
  121.8 1.4 convolution_convert_fusion.6.refs_0_
  123.2 18.9 %shard_map.290 = bf16[512,1024]{1,0:T(8,128)(2,1)} custom-call(bf16[512,1024]{1,0:T(8,128)(2,1)} %convolution_convert_fusion.6.refs_0_), custom_call_target="tpu_custom_call" | custom-call | tf_op jit(solution)/shard_map/pallas_call | solution.py:329
  142.2 1.9 fusion.116
  144.7 5.8 %multiply_convert_fusion.1 = (bf16[512,1024]{1,0:T(8,128)(2,1)S(1)}, f32[512,1024]{1,0:T(8,128)S(1)}, f32[512,1024]{1,0:T(8,128)S(1)}) fusion(f32[1024]{0:T(1024)S(1)} %bitcast.363, bf16[1024,1024]{1,0:T(8,128)(2,1)S(1)} %bitcast.376, f32[1024]{0:T(1024)S(1)} %bitcast.361, f32[1024]{0:T(1024)S(1)} %bitcast.337, f32[512]{0:T(512)S(1)} %add_rsqrt_fusion, ...), kind=kOutput, calls=%fused_computation.77 | convolution fusion | flops 1113587712 | bytes 9461760 | tf_op jit(solution)/shard_map/dot_general | solution.py:852
  150.6 2.0 convert_reduce_fusion.3
  152.5 15.8 %convolution_convert_fusion.1 = bf16[1024,1024]{1,0:T(8,128)(2,1)} fusion(bf16[512,1024]{1,0:T(8,128)(2,1)S(1)} %get-tuple-element.141, f32[1024]{0:T(1024)S(1)} %bitcast.362, f32[1024]{0:T(1024)S(1)} %bitcast.338, f32[512]{0:T(512)S(1)} %add_rsqrt_fusion, f32[512]{0:T(512)S(1)} %broadcast_multiply_fusion.4, f32[1024]{0:T(1024)S(1)} %bitcast.334, ...), kind=kOutput, calls=%fused_computation.105 | convolution fusion | flops 1080033280 | bytes 5263360 | tf_op jit(solution)/shard_map/dot_general | solution.py:36
  168.4 2.2 convolution_convert_fusion.4.refs_1_
  170.6 2.3 convolution_convert_fusion.5.refs_0_
  172.9 31.0 %shard_map.291 = (bf16[512,1024]{1,0:T(8,128)(2,1)}, bf16[512,1024]{1,0:T(8,128)(2,1)}) custom-call(bf16[512,1024]{1,0:T(8,128)(2,1)} %convolution_convert_fusion.5.refs_0_, bf16[512,1024]{1,0:T(8,128)(2,1)} %convolution_convert_fusion.4.refs_1_), custom_call_target="tpu_custom_call" | custom-call | tf_op jit(solution)/shard_map/pallas_call | solution.py:329
  203.9 2.6 fusion.41
  206.6 3.2 multiply_reduce_fusion
  210.8 1.2 convolution_convert_fusion.7.refs_2_
  213.3 1.5 fusion.3
  216.1 1.5 fusion.1
  217.6 1.4 fusion.86
  219.0 1.8 copy.76
  220.8 3.3 fusion.68
  225.3 1.1 pad_maximum_fusion.1
  226.4 2.5 copy.75
  228.9 2.5 fusion.75
  233.3 2.5 copy.74
  235.8 2.1 fusion.89.in_ref
  237.9 14.5 %shard_map.292 = bf16[512,512]{1,0:T(8,128)(2,1)} custom-call(bf16[512,512]{1,0:T(8,128)(2,1)} %fusion.89.in_ref), custom_call_target="tpu_custom_call" | custom-call | tf_op jit(solution)/shard_map/pallas_call | solution.py:247
  252.4 1.5 fusion.92
  254.0 1.6 fusion.119
  255.6 2.3 copy.77
  257.9 3.7 convolution_convert_fusion.2
  261.9 3.7 convolution_convert_fusion.3.refs_0_
  265.6 18.1 %shard_map.293 = bf16[512,1024]{1,0:T(8,128)(2,1)} custom-call(bf16[512,1024]{1,0:T(8,128)(2,1)} %convolution_convert_fusion.3.refs_0_), custom_call_target="tpu_custom_call" | custom-call | tf_op jit(solution)/shard_map/pallas_call | solution.py:329
  283.6 2.8 fusion.42
  287.4 4.2 %convolution_convert_fusion.refs_4_ = bf16[1024,1024]{1,0:T(8,128)(2,1)} fusion(bf16[512,1024]{1,0:T(8,128)(2,1)} %copy-done.36, bf16[1,512,1024]{2,1,0:T(8,128)(2,1)} %param.33, f32[1024]{0:T(1024)S(1)} %bitcast.348), kind=kOutput, calls=%fused_computation.104 | convolution fusion | flops 1076363264 | bytes 4198400 | tf_op jit(solution)/shard_map/dot_general | solution.py:36
  291.5 99.8 %shard_map.294 = (f32[16,128]{1,0:T(8,128)}, f32[128,768]{1,0:T(8,128)}, f32[256,128]{1,0:T(8,128)}, f32[128,1024]{1,0:T(8,128)}, f32[1024,128]{1,0:T(8,128)}) custom-call(f32[8,16,128]{2,1,0:T(8,128)} %pad.19.refs_0_, bf16[8,128,768]{2,1,0:T(8,128)(2,1)} %bitcast.309, bf16[256,1024]{1,0:T(8,128)(2,1)} %convolution_convert_fusion.7.refs_2_, ...), custom_call_target="tpu_custom_call" | custom-call | tf_op jit(solution)/shard_map/pallas_call | solution.py:487
  391.3 1.2 copy.78
  393.4 1.5 slice_bitcast_fusion.2
  396.9 3.4 fusion.30
  (131 shorter events, 24.0 us)
Async XLA Ops:
  0.6 79.2 %copy-start = (bf16[1,512,1024]{2,1,0:T(8,128)(2,1)S(1)}, bf16[1,512,1024]{2,1,0:T(8,128)(2,1)}, u32[]{:S(2)}) copy-start(bf16[1,512,1024]{2,1,0:T(8,128)(2,1)} %param.17) | copy-start | bytes 3145732
  78.8 1.7 copy-start.17
  84.7 1.1 copy-start.18
  104.1 3.7 copy-start.12
  107.9 1.1 copy-start.14
  107.9 3.0 copy-start.2
  109.0 4.8 %copy-start.5 = (f32[4,512,512]{2,1,0:T(8,128)}, f32[4,512,512]{2,1,0:T(8,128)S(1)}, u32[]{:S(2)}) copy-start(f32[4,512,512]{2,1,0:T(8,128)S(1)} %get-tuple-element.132) | copy-start | bytes 12582916
  114.0 3.4 copy-start.29
  117.5 4.2 %copy-start.31 = (bf16[512,256]{0,1:T(8,128)(2,1)}, bf16[512,256]{0,1:T(8,128)(2,1)S(1)}, u32[]{:S(2)}) copy-start(bf16[512,256]{0,1:T(8,128)(2,1)S(1)} %copy.66) | copy-start | bytes 786436
  117.6 4.2 %copy-start.16 = (bf16[256,1024]{1,0:T(8,128)(2,1)S(1)}, bf16[256,1024]{1,0:T(8,128)(2,1)}, u32[]{:S(2)}) copy-start(bf16[256,1024]{1,0:T(8,128)(2,1)} %get-tuple-element.30) | copy-start | bytes 1572868
  121.8 22.3 %copy-start.21 = (bf16[512,4,64]{0,2,1:T(8,128)(2,1)}, bf16[512,4,64]{0,2,1:T(8,128)(2,1)S(1)}, u32[]{:S(2)}) copy-start(bf16[512,4,64]{0,2,1:T(8,128)(2,1)S(1)} %get-tuple-element.135) | copy-start | bytes 786436
  142.2 1.9 copy-start.1
  142.2 2.5 copy-start.34
  144.7 5.8 %copy-start.19 = (bf16[1,512,1024]{2,1,0:T(8,128)(2,1)S(1)}, bf16[1,512,1024]{2,1,0:T(8,128)(2,1)}, u32[]{:S(2)}) copy-start(bf16[1,512,1024]{2,1,0:T(8,128)(2,1)} %param.33) | copy-start | bytes 3145732
  144.7 5.8 %copy-start.35 = (bf16[1024,1024]{1,0:T(8,128)(2,1)S(1)}, bf16[1024,1024]{1,0:T(8,128)(2,1)}, u32[]{:S(2)}) copy-start(bf16[1024,1024]{1,0:T(8,128)(2,1)} %get-tuple-element.32) | copy-start | bytes 6291460
  150.5 17.9 %copy-start.36 = (bf16[512,1024]{1,0:T(8,128)(2,1)}, bf16[512,1024]{1,0:T(8,128)(2,1)S(1)}, u32[]{:S(2)}) copy-start(bf16[512,1024]{1,0:T(8,128)(2,1)S(1)} %get-tuple-element.93) | copy-start | bytes 3145732
  203.9 2.7 copy-start.11
  203.9 2.7 copy-start.20
  209.9 0.9 copy-start.22
  209.9 2.2 copy-start.26
  209.9 2.7 copy-start.30
  210.8 2.4 copy-start.6
  212.6 2.7 copy-start.27
  213.3 1.5 copy-start.15
  213.3 2.3 copy-start.3
  214.8 2.8 copy-start.7
  214.8 1.3 copy-start.32
  216.1 1.5 copy-start.13
  217.6 1.4 copy-start.8
  220.8 3.5 copy-start.4
  220.8 3.5 copy-start.28
  228.9 2.5 copy-start.9
  252.4 1.6 copy-start.23
  257.9 3.7 copy-start.10
  396.9 3.4 copy-start.33
  396.9 4.1 %copy-start.25 = (f32[128,1024]{1,0:T(8,128)S(1)}, f32[128,1024]{1,0:T(8,128)}, u32[]{:S(2)}) copy-start(f32[128,1024]{1,0:T(8,128)} %get-tuple-element.171) | copy-start | bytes 1572868
  396.9 4.9 %copy-start.24 = (f32[1024,128]{1,0:T(8,128)S(1)}, f32[1024,128]{1,0:T(8,128)}, u32[]{:S(2)}) copy-start(f32[1024,128]{1,0:T(8,128)} %get-tuple-element.173) | copy-start | bytes 1572868

commit v2 on v1

--- a/solution.py
+++ b/solution.py
@@ -118,9 +118,45 @@
     return ref.at[:, pl.ds(pl.multiple_of(owner * width, width), width)]
 
 
-def gather_kernel(line, count, *refs):
-    ins, outs = refs[:count], refs[count : 2 * count]
-    send, recv, local = refs[2 * count :]
+def attend_head(head, query_ref, near_ref, far_ref, near_mask, far_mask, attn_ref, log_ref):
+    rows, width = query_ref.shape
+    block = math.gcd(rows, 256)
+    at = slice(head * HEAD_DIM, (head + 1) * HEAD_DIM)
+    value_at = slice(width + head * HEAD_DIM, width + (head + 1) * HEAD_DIM)
+
+    def body(i, carry):
+        rows_at = pl.ds(pl.multiple_of(i * block, block), block)
+        query = query_ref[rows_at, at]
+        near = contract_cols(query, near_ref[:, at]) * HEAD_DIM ** (-0.5)
+        far = contract_cols(query, far_ref[:, at]) * HEAD_DIM ** (-0.5)
+        near = jnp.where(near_mask[...] > 0, near, NEGATIVE)
+        far = jnp.where(far_mask[...] > 0, far, NEGATIVE)
+        highest = jnp.maximum(
+            jnp.max(near, axis=-1, keepdims=True), jnp.max(far, axis=-1, keepdims=True)
+        )
+        near = jnp.exp(near - highest)
+        far = jnp.exp(far - highest)
+        total = jnp.sum(near, axis=-1, keepdims=True) + jnp.sum(far, axis=-1, keepdims=True)
+        out = jnp.dot(
+            near.astype(jnp.bfloat16), near_ref[:, value_at], preferred_element_type=jnp.float32
+        ) + jnp.dot(
+            far.astype(jnp.bfloat16), far_ref[:, value_at], preferred_element_type=jnp.float32
+        )
+        attn_ref[rows_at, at] = out / total
+        log_ref[rows_at, head : head + 1] = highest + jnp.log(total)
+        return carry
+
+    lax.fori_loop(0, rows // block, body, 0)
+
+
+def gather_kernel(line, count, attend_too, *refs):
+    extra_in = 4 if attend_too else 0
+    extra_out = 3 if attend_too else 0
+    ins, rest = refs[:count], refs[count:]
+    given, rest = rest[:extra_in], rest[extra_in:]
+    outs, rest = rest[:count], rest[count:]
+    made, rest = rest[:extra_out], rest[extra_out:]
+    send, recv, local = rest[:3]
     here = lax.axis_index("dp")
     side = lax.axis_index("context")
     cross = 2 * (line - 1)
@@ -152,6 +188,13 @@
         )
 
     greet_line(line)
+    heads = []
+    if attend_too:
+        query_ref, near_ref, near_mask, far_mask = given
+        far_ref, attn_ref, log_ref = made
+        swap_copy = remote(near_ref, far_ref, rest[3], rest[4], {"context": 1 - side})
+        swap_copy.start()
+        heads = list(range(query_ref.shape[1] // HEAD_DIM))
     for a in range(count):
 
         @pl.when(here < line - 1)
@@ -186,6 +229,15 @@
                     down(a, s, here + s).start()
 
                 over(a, here + s, False).start()
+
+        if attend_too and s == 1:
+            swap_copy.wait()
+        now = heads[:2] if s < line - 1 else heads
+        heads = heads[len(now) :]
+        for head in now:
+            attend_head(
+                head, query_ref, near_ref, far_ref, near_mask, far_mask, attn_ref, log_ref
+            )
 
     for a in range(count):
         pltpu.make_async_copy(ins[a], part(a, here, side), local.at[a]).wait()
@@ -209,7 +261,7 @@
                 down(a, s, here + s).wait_send()
 
 
-def gather_parts(arrays, stacked, line, ident):
+def gather_parts(arrays, stacked, line, ident, attend_args=()):
     owners = line * 2
     shapes = []
     for array, stack in zip(arrays, stacked):
@@ -220,18 +272,31 @@
         shapes.append(jax.ShapeDtypeStruct(shape, array.dtype))
     count = len(arrays)
     slots = 2 * (line - 1) + line
+    anywhere = pl.BlockSpec(memory_space=pl.ANY)
+    in_vmem = pl.BlockSpec(memory_space=pltpu.VMEM)
+    extra_shapes = []
+    extra_sems = []
+    if attend_args:
+        query, key_value = attend_args[:2]
+        extra_shapes = [
+            jax.ShapeDtypeStruct(key_value.shape, key_value.dtype),
+            jax.ShapeDtypeStruct(query.shape, jnp.float32),
+            jax.ShapeDtypeStruct((query.shape[0], 128), jnp.float32),
+        ]
+        extra_sems = [pltpu.SemaphoreType.DMA, pltpu.SemaphoreType.DMA]
     return pl.pallas_call(
-        functools.partial(gather_kernel, line, count),
-        out_shape=tuple(shapes),
-        in_specs=[pl.BlockSpec(memory_space=pl.ANY)] * count,
-        out_specs=tuple([pl.BlockSpec(memory_space=pl.ANY)] * count),
+        functools.partial(gather_kernel, line, count, bool(attend_args)),
+        out_shape=tuple(shapes + extra_shapes),
+        in_specs=[anywhere] * count + [in_vmem] * len(attend_args),
+        out_specs=tuple([anywhere] * count + [in_vmem] * len(extra_shapes)),
         scratch_shapes=[
             pltpu.SemaphoreType.DMA((count, slots)),
             pltpu.SemaphoreType.DMA((count, slots)),
             pltpu.SemaphoreType.DMA((count,)),
-        ],
+        ]
+        + extra_sems,
         compiler_params=params(ident),
-    )(*arrays)
+    )(*arrays, *attend_args)
 
 
 def swap_kernel(in_ref, out_ref, send, recv):
@@ -397,10 +462,15 @@
         )
 
     greet_line(line)
-    for k in range(line // 2):
+    order = [
+        jnp.where(here < 2, 3, 0),
+        jnp.where(here == 0, 2, jnp.where(here == 1, 0, jnp.where(here == 2, 3, 1))),
+        jnp.where(here == 0, 1, jnp.where(here == 1, 2, jnp.where(here == 2, 1, 2))),
+        here,
+    ]
+    for row in order:
         for a in range(count):
-            over(a, line - 1 - k).start()
-            over(a, k).start()
+            over(a, row).start()
     for k in range(line - 1):
         for a in range(count):
             high, low = line - 1 - k, k
@@ -767,14 +837,10 @@
         1,
         jnp.bfloat16,
     )[0]
-    pack_full, qkv_full, out_full, fc1_full, fc2_full = gather_parts(
-        [packed, w_qkv.reshape(w_qkv.shape[0], -1), w_out, w_fc1, w_fc2],
-        [True, True, False, True, False],
-        line,
-        1,
+    pack_full, qkv_full = gather_parts(
+        [packed, w_qkv.reshape(w_qkv.shape[0], -1)], [True, True], line, 1
     )
     qkv_full = qkv_full.reshape((-1,) + w_qkv.shape[1:])
-    fc1_full = fc1_full.reshape(-1, fc1_full.shape[-1])
     (
         gain_one,
         shift_one,
@@ -820,25 +886,26 @@
     values = (projected[:, 2] + qv_float[1]).astype(jnp.bfloat16)
     query_heads = queries.reshape(row_count, head_count, HEAD_DIM)
     key_value = jnp.concatenate([key_rows, values], axis=1)
-    other = swap(key_value, 2)
+    far_mask = lax.dynamic_slice_in_dim(full_mask, (1 - side) * row_count, row_count, axis=0)
+    out_full, fc1_full, fc2_full, other, attn_flat, log_flat = gather_parts(
+        [w_out, w_fc1, w_fc2],
+        [False, True, False],
+        line,
+        2,
+        (
+            queries,
+            key_value,
+            mask_row.astype(jnp.float32)[None],
+            far_mask.astype(jnp.float32)[None],
+        ),
+    )
+    fc1_full = fc1_full.reshape(-1, fc1_full.shape[-1])
     pair = jnp.where(
         side == 0, jnp.concatenate([key_value, other]), jnp.concatenate([other, key_value])
     )
     back_keys, back_values = pair[:, :local_width], pair[:, local_width:]
-    start_carry = (
-        jnp.full((row_count, head_count, 1), NEGATIVE, jnp.float32),
-        jnp.zeros((row_count, head_count, 1), jnp.float32),
-        jnp.zeros((row_count, head_count, HEAD_DIM), jnp.float32),
-    )
-    running_max, running_total, running_sum = attend(
-        start_carry,
-        query_heads,
-        back_keys,
-        back_values,
-        full_mask,
-    )
-    attn_heads = running_sum / running_total
-    log_total = running_max + jnp.log(running_total)
+    attn_heads = attn_flat.reshape(row_count, head_count, HEAD_DIM)
+    log_total = log_flat[:, :head_count].reshape(row_count, head_count, 1)
     attended = attn_heads.reshape(row_count, local_width).astype(jnp.bfloat16)
     branch = (
         tensor_sum(

time: 404 us -> 385 us (0.953); the launches traced: 403 us -> 378 us
  Pallas kernels: 268 us -> 252 us
  matrix products: 69.2 us -> 57.6 us
    pallas_call x1, Pallas kernels: 99.8 us -> 82.3 us  [scatter_parts(): pl.pallas_call(functools.partial(scatter_kernel, line, count), out_shape=...]
    pallas_call x1 -> x2, Pallas kernels: 72.6 us -> 87.4 us  [gather_parts(): pl.pallas_call(functools.partial(gather_kernel, line, count, bool(attend_...]
    dot_general x4, matrix products: 24.9 us -> 10.6 us  [contract_rows(): lax.dot_general(first_matrix, second_matrix, (((0,), (0,)), ((), ())), pr...]
    pallas_call x2 -> x1, Pallas kernels: 27.7 us -> 14.5 us  [swap(): pl.pallas_call(swap_kernel, out_shape=jax.ShapeDtypeStruct(array.shape, a...]
    dot_general x4 -> x2, matrix products: 11.6 us -> 5.4 us  [on_device_line(): jnp.einsum('rhe,nhe->rhn', query_heads, key_block, preferred_element_type...]
    dot_general x2, matrix products: 2.99 us -> 7.39 us  [on_device_line(): jnp.einsum('rhe,nhe->rhn', grad_attn_heads, value_block, preferred_elemen...]
    unnamed x81 -> x79, local copies, waits for them, and re-layouts: 10.1 us -> 8.66 us
where the time goes in v2:
time: 385 us; the launch traced here: 378 us
  Pallas kernels  252 us (65%)
  matrix products  57.6 us (15%)
  other arithmetic  33.7 us (9%)
  local copies, waits for them, and re-layouts  32.5 us (8%)
    pallas_call x2, Pallas kernels, gather_parts(): pl.pallas_call(functools.partial(gather_kernel, line, count, bool(attend_...  87.4 us
    pallas_call x1, Pallas kernels, scatter_parts(): pl.pallas_call(functools.partial(scatter_kernel, line, count), out_shape=...  82.3 us
    pallas_call x3, Pallas kernels, tensor_sum(): pl.pallas_call(functools.partial(tensor_sum_kernel, count), out_shape=tup...  68.1 us
    pallas_call x1, Pallas kernels, swap(): pl.pallas_call(swap_kernel, out_shape=jax.ShapeDtypeStruct(array.shape, a...  14.5 us
    dot_general x4, matrix products, contract_rows(): lax.dot_general(first_matrix, second_matrix, (((0,), (0,)), ((), ())), pr...  10.6 us
    dot_general x4, matrix products, contract_cols(): lax.dot_general(first_matrix, second_matrix, (((1,), (1,)), ((), ())), pr...  9.42 us
    unnamed x79, local copies, waits for them, and re-layouts  8.66 us

profile of v2, /device:TPU:16, one launch (start us, length us, event | category | flops | bytes accessed | tf_op | source)
XLA Modules:
  0.0 377.7 jit_solution(15472724480608974117)
XLA Ops:
  0.7 1.2 copy.57
  4.1 1.5 concatenate.25
  6.2 21.8 %shard_map.288 = (bf16[8,16,128]{2,1,0:T(8,128)(2,1)}, bf16[8,128,768]{2,1,0:T(8,128)(2,1)}) custom-call(bf16[16,128]{1,0:T(8,128)(2,1)} %pad_bitcast_fusion.refs_0_, bf16[128,768]{1,0:T(8,128)(2,1)} %copy.58.refs_1_), custom_call_target="tpu_custom_call" | custom-call | tf_op jit(solution)/shard_map/pallas_call | solution.py:287
  29.1 1.4 convert_reduce_fusion.2
  31.0 1.6 copy.59
  32.6 3.7 fusion.66
  37.3 2.0 fusion.75
  43.1 65.5 %shard_map.289 = (bf16[256,1024]{1,0:T(8,128)(2,1)}, bf16[8,128,1024]{2,1,0:T(8,128)(2,1)}, bf16[1024,1024]{1,0:T(8,128)(2,1)}, bf16[512,512]{1,0:T(8,128)(2,1)}...) custom-call(bf16[256,128]{1,0:T(8,128)(2,1)} %refs_0_.1, bf16[128,1024]{1,0:T(8,128)(2,1)} %refs_1_.1, ...), custom_call_target="tpu_custom_call" | custom-call | tf_op jit(solution)/shard_map/pallas_call | solution.py:287
  108.7 2.6 convolution_convert_fusion.6.refs_0_
  111.3 18.9 %shard_map.290 = bf16[512,1024]{1,0:T(8,128)(2,1)} custom-call(bf16[512,1024]{1,0:T(8,128)(2,1)} %convolution_convert_fusion.6.refs_0_), custom_call_target="tpu_custom_call" | custom-call | tf_op jit(solution)/shard_map/pallas_call | solution.py:394
  130.2 1.9 fusion.84
  132.8 7.2 %multiply_convert_fusion.1 = (bf16[512,1024]{1,0:T(8,128)(2,1)}, f32[512,1024]{1,0:T(8,128)S(1)}, f32[512,1024]{1,0:T(8,128)S(1)}) fusion(f32[1024]{0:T(1024)S(1)} %bitcast.321, bf16[1024,1024]{1,0:T(8,128)(2,1)S(1)} %bitcast.334, f32[1024]{0:T(1024)S(1)} %bitcast.319, f32[1024]{0:T(1024)S(1)} %bitcast.292, f32[512]{0:T(512)S(1)} %add_rsqrt_fusion, ...), kind=kOutput, calls=%fused_computation.67 | convolution fusion | flops 1113587712 | bytes 9461760 | tf_op jit(solution)/shard_map/dot_general | solution.py:919
  139.9 2.0 convert_reduce_fusion.3
  142.0 3.0 convolution_convert_fusion.1
  147.6 1.1 add_convert_fusion.3
  148.8 2.7 fusion.91
  151.5 2.2 convolution_convert_fusion.4.refs_1_
  153.8 2.3 convolution_convert_fusion.5.refs_0_
  156.0 31.1 %shard_map.291 = (bf16[512,1024]{1,0:T(8,128)(2,1)}, bf16[512,1024]{1,0:T(8,128)(2,1)}) custom-call(bf16[512,1024]{1,0:T(8,128)(2,1)} %convolution_convert_fusion.5.refs_0_, bf16[512,1024]{1,0:T(8,128)(2,1)} %convolution_convert_fusion.4.refs_1_), custom_call_target="tpu_custom_call" | custom-call | tf_op jit(solution)/shard_map/pallas_call | solution.py:394
  187.1 2.6 fusion.35
  189.8 3.5 multiply_reduce_fusion
  193.4 1.3 copy-done.2
  196.0 1.7 multiply_reduce_fusion.2
  200.3 3.7 fusion.5
  204.1 1.3 copy-done.4
  205.3 1.3 fusion.92
  206.8 2.7 fusion.93
  209.7 3.7 fusion.1
  213.4 1.4 copy-done.5
  216.0 3.2 fusion.50
  221.4 1.6 copy.77
  223.0 2.5 fusion.57
  227.3 2.5 copy.76
  229.9 1.9 fusion.62.in_ref
  231.8 14.5 %shard_map.292 = bf16[512,512]{1,0:T(8,128)(2,1)} custom-call(bf16[512,512]{1,0:T(8,128)(2,1)} %fusion.62.in_ref), custom_call_target="tpu_custom_call" | custom-call | tf_op jit(solution)/shard_map/pallas_call | solution.py:312
  246.3 1.4 fusion.65
  247.7 1.4 fusion.87
  249.1 1.2 copy.79
  250.3 3.7 convolution_convert_fusion.2
  254.3 3.4 convolution_convert_fusion.3.refs_0_
  257.8 18.1 %shard_map.293 = bf16[512,1024]{1,0:T(8,128)(2,1)} custom-call(bf16[512,1024]{1,0:T(8,128)(2,1)} %convolution_convert_fusion.3.refs_0_), custom_call_target="tpu_custom_call" | custom-call | tf_op jit(solution)/shard_map/pallas_call | solution.py:394
  275.9 3.1 fusion.36
  279.7 1.3 convolution_convert_fusion.7.refs_2_
  281.0 2.6 convolution_convert_fusion.refs_4_
  283.6 82.3 %shard_map.294 = (f32[16,128]{1,0:T(8,128)}, f32[128,768]{1,0:T(8,128)}, f32[256,128]{1,0:T(8,128)}, f32[128,1024]{1,0:T(8,128)}, f32[1024,128]{1,0:T(8,128)}) custom-call(f32[8,16,128]{2,1,0:T(8,128)} %pad.19.refs_0_, bf16[8,128,768]{2,1,0:T(8,128)(2,1)} %bitcast.267, bf16[256,1024]{1,0:T(8,128)(2,1)} %convolution_convert_fusion.7.refs_2_, ...), custom_call_target="tpu_custom_call" | custom-call | tf_op jit(solution)/shard_map/pallas_call | solution.py:557
  366.0 1.2 copy.80
  368.0 1.5 slice_bitcast_fusion.3
  371.6 3.4 fusion.24
  (131 shorter events, 28.5 us)
Async XLA Ops:
  0.6 29.9 %copy-start = (bf16[1,512,1024]{2,1,0:T(8,128)(2,1)S(1)}, bf16[1,512,1024]{2,1,0:T(8,128)(2,1)}, u32[]{:S(2)}) copy-start(bf16[1,512,1024]{2,1,0:T(8,128)(2,1)} %param.17) | copy-start | bytes 3145732
  28.0 2.9 copy-start.13
  36.3 6.2 %copy-start.28 = (s32[1,512]{1,0:T(1,128)S(1)}, s32[1,512]{1,0:T(1,128)}, u32[]{:S(2)}) copy-start(s32[1,512]{1,0:T(1,128)} %param.18) | copy-start | bytes 6148
  130.2 1.9 copy-start.1
  130.2 2.5 copy-start.29
  132.7 7.2 %copy-start.14 = (bf16[1,512,1024]{2,1,0:T(8,128)(2,1)S(1)}, bf16[1,512,1024]{2,1,0:T(8,128)(2,1)}, u32[]{:S(2)}) copy-start(bf16[1,512,1024]{2,1,0:T(8,128)(2,1)} %param.33) | copy-start | bytes 3145732
  132.8 7.2 %copy-start.31 = (bf16[1024,1024]{1,0:T(8,128)(2,1)S(1)}, bf16[1024,1024]{1,0:T(8,128)(2,1)}, u32[]{:S(2)}) copy-start(bf16[1024,1024]{1,0:T(8,128)(2,1)} %get-tuple-element.36) | copy-start | bytes 6291460
  141.9 3.0 copy-start.35
  141.9 3.0 copy-start.22
  145.4 1.2 slice-start
  148.8 2.7 copy-start.32
  148.8 2.7 copy-start.33
  151.5 2.2 copy-start.30
  151.5 2.2 copy-start.36
  187.1 2.7 copy-start.10
  187.1 2.7 copy-start.15
  187.1 2.7 copy-start.17
  193.3 1.3 copy-start.2
  193.4 1.7 copy-start.7
  196.0 1.8 copy-start.20
  197.8 2.6 copy-start.25
  204.0 1.3 copy-start.4
  205.3 1.3 copy-start.19
  206.8 2.9 copy-start.26
  209.7 5.1 %copy-start.12 = (f32[4,64,512]{2,1,0:T(8,128)S(1)}, f32[4,64,512]{2,1,0:T(8,128)}, u32[]{:S(2)}) copy-start(f32[4,64,512]{2,1,0:T(8,128)} %fusion.92) | copy-start | bytes 1572868
  213.4 1.4 copy-start.5
  216.0 3.4 copy-start.11
  223.0 2.5 copy-start.6
  246.3 1.4 copy-start.18
  250.3 3.7 copy-start.9
  250.3 4.1 %copy-start.21 = (bf16[512,3,256]{0,2,1:T(8,128)(2,1)S(1)}, bf16[512,3,256]{0,2,1:T(8,128)(2,1)}, u32[]{:S(2)}) copy-start(bf16[512,3,256]{0,2,1:T(8,128)(2,1)} %copy.79) | copy-start | bytes 2359300
  257.8 21.9 %copy-start.8 = (f32[512,256]{1,0:T(8,128)S(1)}, f32[512,256]{1,0:T(8,128)}, u32[]{:S(2)}) copy-start(f32[512,256]{1,0:T(8,128)} %get-tuple-element.33) | copy-start | bytes 1572868
  279.0 1.9 copy-start.16
  279.1 1.9 copy-start.34
  283.6 88.0 %copy-start.3 = (f32[512,1024]{1,0:T(8,128)S(1)}, f32[512,1024]{1,0:T(8,128)}, u32[]{:S(2)}) copy-start(f32[512,1024]{1,0:T(8,128)} %copy-done.2) | copy-start | bytes 6291460
  371.6 3.4 copy-start.27
  371.6 4.1 %copy-start.24 = (f32[128,1024]{1,0:T(8,128)S(1)}, f32[128,1024]{1,0:T(8,128)}, u32[]{:S(2)}) copy-start(f32[128,1024]{1,0:T(8,128)} %get-tuple-element.166) | copy-start | bytes 1572868
  371.6 4.9 %copy-start.23 = (f32[1024,128]{1,0:T(8,128)S(1)}, f32[1024,128]{1,0:T(8,128)}, u32[]{:S(2)}) copy-start(f32[1024,128]{1,0:T(8,128)} %get-tuple-element.168) | copy-start | bytes 1572868
